TPU v7x, 256 devices: a whole 4x4x8 slice. The times are simulated.
256 devices in a mesh: gx: 16 (over y_hi, x, core), gy: 16 (over y_lo, z).
Axes of the slice: x: 4, y: 4 (y_hi: 2, y_lo: 2; y = y_hi * 2 + y_lo), z: 8, core: 2. Of those that a mesh axis runs over, the one named last changes fastest.
Arguments:
- velocity: bfloat16 [4, 2, 256, 2048], P(None, None, 'gy', 'gx'), may hold values from -6 to 6
- conv_one: bfloat16 [2, 5, 5, 128], replicated, may hold values from -0.875 to 0.875
- bias_one: float32 [128], replicated, may hold values from -3 to 3
- conv_two: bfloat16 [5, 5, 64, 128], replicated, may hold values from -0.109375 to 0.109375
- bias_two: float32 [64], replicated, may hold values from -3 to 3
- conv_three: bfloat16 [2, 3, 3, 64], replicated, may hold values from -0.25 to 0.25
- bias_three: float32 [2], replicated, may hold values from -3 to 3
- drop_one: int32 [2, 128], replicated, may hold values 0 or 1
- drop_two: int32 [2, 64], replicated, may hold values 0 or 1
- thickness: float32 [4], replicated, may hold values from 0.5 to 2
- eta_old: float32 [256, 2048], P('gy', 'gx'), may hold values from -6 to 6
- face_coef: float32 [2, 256, 2048], P(None, 'gy', 'gx'), may hold values from 0.5 to 5
- storage: float32 [256, 2048], P('gy', 'gx'), may hold values from 0.05 to 0.5
- ocean: int32 [256, 2048], P('gy', 'gx'), may hold values 0 or 1
Outputs:
- forcing: float32 [4, 2, 256, 2048], P(None, None, 'gy', 'gx')
- eta_new: float32 [256, 2048], P('gy', 'gx')
Inputs may be any that keep to these rules, and one draw needn't show every extreme that they name: 1 marks an ocean column, 0 land. `drop_one`: 1 keeps a channel, 0 drops it. `drop_two`: 1 keeps a channel, 0 drops it.
All inputs are finite; a program needn't handle non-finite values. No bound on the sum of `ocean` on one device may be relied on, other than what follows from the above.
Results may differ from a plain program's by a relative error of at most 0.0056.
Values may be sent and summed in bfloat16 or wider, within the bound.
A program may use at most 64 MiB of HBM per device.

v0:
```python
import jax
import jax.numpy as jnp
from jax import lax
from jax.sharding import PartitionSpec as P

ITERS = 3


keep_rate = 0.75


def with_halo(block, sides, width):
    for axis, dim in sides:
        count = lax.axis_size(axis)
        forward = [(i, i + 1) for i in range(count - 1)]
        forward.append((count - 1, 0))
        backward = [(target, source) for source, target in forward]
        low = lax.ppermute(
            lax.slice_in_dim(block, block.shape[dim] - width, None, axis=dim), axis, forward
        )
        high = lax.ppermute(lax.slice_in_dim(block, 0, width, axis=dim), axis, backward)
        block = jnp.concatenate([low, block, high], axis=dim)
    return block


def passed_along(value, axis, steps):
    count = lax.axis_size(axis)
    pairs = [(source, (source + steps) % count) for source in range(count)]
    return lax.ppermute(value, axis, pairs)


def shifted(x, axis, by):
    count = lax.axis_size(axis)
    pairs = [(i, i + by) for i in range(count) if 0 <= i + by < count]
    return lax.ppermute(x, axis, pairs)


def convolve(field, kernel, layout):
    return lax.conv_general_dilated(
        field,
        kernel,
        (1, 1),
        "VALID",
        dimension_numbers=("NCHW", layout, "NCHW"),
        preferred_element_type=jnp.float32,
    )


def clear_rows(padded, width):
    rows = padded.shape[-2]
    count = rows - 2 * width
    start = lax.axis_index("gy") * count - width
    position = start + lax.iota(jnp.int32, rows)
    inside = (position >= 0) & (position < count * lax.axis_size("gy"))
    return jnp.where(inside[:, None], padded, jnp.zeros((), padded.dtype))


def neighbours(padded):
    return (padded[1:-1, 2:], padded[1:-1, :-2], padded[2:, 1:-1], padded[:-2, 1:-1])


def squares(residual):
    return lax.psum(jnp.sum(residual * residual), ("gx", "gy"))


def body(
    velocity,
    conv_one,
    bias_one,
    conv_two,
    bias_two,
    conv_three,
    bias_three,
    drop_one,
    drop_two,
    thickness,
    eta_old,
    face_coef,
    storage,
    ocean,
):
    levels = velocity.shape[0]
    masks = drop_one.shape[0]
    keep_first = drop_one.astype(jnp.float32) / keep_rate
    keep_second = jnp.repeat(drop_two.astype(jnp.float32) / keep_rate, levels, axis=0)
    reach_wide = conv_two.shape[0] // 2
    reach_narrow = conv_three.shape[1] // 2
    padded = clear_rows(with_halo(velocity, (("gx", 3), ("gy", 2)), reach_wide), reach_wide)
    first = convolve(padded, conv_one, "IHWO") + bias_one[None, :, None, None]
    scaled = jax.nn.relu(first)[None] * keep_first[:, None, :, None, None]
    hidden_one = scaled.reshape((masks * levels,) + first.shape[1:]).astype(jnp.bfloat16)
    padded_one = clear_rows(with_halo(hidden_one, (("gx", 3), ("gy", 2)), reach_wide), reach_wide)
    second = convolve(padded_one, conv_two, "HWOI") + bias_two[None, :, None, None]
    hidden_two = (jax.nn.relu(second) * keep_second[:, :, None, None]).astype(jnp.bfloat16)
    padded_two = clear_rows(
        with_halo(hidden_two, (("gx", 3), ("gy", 2)), reach_narrow), reach_narrow
    )
    outputs = convolve(padded_two, conv_three, "OHWI") + bias_three[None, :, None, None]
    forcing = jnp.sum(outputs.reshape((masks, levels) + outputs.shape[1:]), axis=0) / masks
    moved = velocity.astype(jnp.float32) + forcing
    zonal = jnp.sum(thickness[:, None, None] * moved[:, 0], axis=0)
    merid = jnp.sum(thickness[:, None, None] * moved[:, 1], axis=0)
    sea_here = ocean.astype(jnp.float32)
    stacked = jnp.stack([sea_here, face_coef[0], face_coef[1]])
    coef_pad = clear_rows(with_halo(stacked, (("gx", 2), ("gy", 1)), 1), 1)
    sea_east, sea_west, sea_north, sea_south = neighbours(coef_pad[0])
    open_east = sea_here * sea_east
    open_west = sea_here * sea_west
    open_north = sea_here * sea_north
    open_south = sea_here * sea_south
    coef_east = face_coef[0] * open_east
    coef_west = coef_pad[1, 1:-1, :-2] * open_west
    coef_north = face_coef[1] * open_north
    coef_south = coef_pad[2, :-2, 1:-1] * open_south
    flux_east = zonal * open_east
    flux_north = merid * open_north
    west_column = passed_along(flux_east[:, -1:], "gx", 1)
    south_row = shifted(flux_north[-1:, :], "gy", 1)
    flux_west = jnp.concatenate([west_column, flux_east[:, :-1]], axis=1)
    flux_south = jnp.concatenate([south_row, flux_north[:-1, :]], axis=0)
    diverge = flux_east - flux_west + flux_north - flux_south
    right = storage * eta_old - diverge

    def operate(field):
        padded_field = clear_rows(with_halo(field, (("gx", 1), ("gy", 0)), 1), 1)
        to_east, to_west, to_north, to_south = neighbours(padded_field)
        return (
            storage * field
            + coef_east * (field - to_east)
            + coef_west * (field - to_west)
            + coef_north * (field - to_north)
            + coef_south * (field - to_south)
        )

    solution = eta_old
    residual = right - operate(eta_old)
    direction = residual
    norm_now = squares(residual)
    for number in range(ITERS):
        image = operate(direction)
        alpha = norm_now / lax.psum(jnp.sum(direction * image), ("gx", "gy"))
        solution = solution + alpha * direction
        residual = residual - alpha * image
        if number + 1 < ITERS:
            norm_next = squares(residual)
            direction = residual + norm_next / norm_now * direction
            norm_now = norm_next
    return (forcing, solution)


def solution(mesh):
    in_specs = (
        P(None, None, "gy", "gx"),
        P(),
        P(),
        P(),
        P(),
        P(),
        P(),
        P(),
        P(),
        P(),
        P("gy", "gx"),
        P(None, "gy", "gx"),
        P("gy", "gx"),
        P("gy", "gx"),
    )
    out_specs = (P(None, None, "gy", "gx"), P("gy", "gx"))
    return jax.shard_map(body, mesh=mesh, in_specs=in_specs, out_specs=out_specs, check_vma=False)
```

profile of v0, /device:TPU:1, one launch (start us, length us, event | category | flops | bytes accessed | tf_op | source)
XLA Modules:
  0.0 642.2 jit_solution(12915195932462659190)
XLA Ops:
  1.6 2.6 collective-permute-start
  10.8 5.3 collective-permute-start.3
  18.7 2.7 add_maximum_fusion
  21.5 2.6 copy.21
  24.4 2.7 copy.22
  27.1 4.6 mul.202
  31.6 4.4 multiply_convert_fusion.1
  36.1 2.0 copy-done.1
  39.0 3.1 collective-permute-start.5
  42.2 5.3 collective-permute-start.19
  49.1 4.2 collective-permute-start.7
  53.3 5.6 collective-permute-start.13
  59.0 3.6 collective-permute-start.21
  62.8 3.6 collective-permute-start.15
  66.4 28.3 %multiply_convert_fusion = bf16[8,64,16,128]{1,0,3,2:T(8,128)(2,1)S(1)} fusion(bf16[5,5,64,128]{3,2,1,0:T(8,128)(2,1)S(1)} %copy-done, bf16[8,128,2,132]{1,0,3,2:T(8,128)(2,1)S(1)} %collective-permute-done.7, bf16[8,128,16,2]{1,0,3,2:T(8,128)(2,1)S(1)} %collective-permute-done.5, bf16[8,128,16,128]{1,0,3,2:T(8,128)(2,1)S(1)} %copy-done.2, ...), kind=kOutput, calls=%fused_computation | convolution fusion | flops 6728597504 | bytes 7915796 | tf_op jit(solution)/shard_map/conv_general_dilated | solution.py:39
  94.9 3.2 collective-permute-start.9
  99.1 3.6 collective-permute-start.11
  102.7 3.9 collective-permute-done.10
  106.6 92.8 %fusion.22 = f32[8,2,16,128]{0,1,3,2:T(2,128)S(1)} fusion(bf16[2,3,3,64]{3,0,2,1:T(2,128)(2,1)S(1)} %copy-done.10, bf16[8,64,1,130]{1,0,3,2:T(8,128)(2,1)S(1)} %collective-permute-done.11, bf16[8,64,16,1]{1,0,3,2:T(8,128)(2,1)S(1)} %collective-permute-done.9, bf16[8,64,16,128]{1,0,3,2:T(8,128)(2,1)S(1)} %multiply_convert_fusion, ...), kind=kOutput, calls=%fused_computation.28 | convolution fusion | flops 43771904 | bytes 2529562 | tf_op jit(solution)/shard_map/conv_general_dilated | solution.py:39
  203.0 5.9 collective-permute-done.16
  209.1 6.1 collective-permute-start.23
  216.1 3.9 collective-permute-start.25
  222.0 83.9 %all-reduce = (f32[]{:T(128)}, f32[]{:T(128)}) all-reduce(f32[]{:T(128)} %get-tuple-element.5, f32[]{:T(128)} %get-tuple-element.4), channel_id=1, replica_groups=mesh['gx'=16,'gy'=16] {'gx','gy'}, use_global_device_ids=true, to_apply=%region_4.5 | all-reduce | flops 2 | bytes 16 | tf_op jit(solution)/shard_map/psum | solution.py:63
  307.8 73.4 %psum.44 = f32[]{:T(128)} all-reduce(f32[]{:T(128)} %get-tuple-element.10), channel_id=1, replica_groups=mesh['gx'=16,'gy'=16] {'gx','gy'}, use_global_device_ids=true, to_apply=%region_8.9 | all-reduce | flops 1 | bytes 8 | tf_op jit(solution)/shard_map/psum | solution.py:63
  384.7 2.3 collective-permute-done.27
  387.0 1.8 collective-permute-start.28
  388.8 1.8 collective-permute-start.29
  392.4 80.6 %psum.45 = f32[]{:T(128)} all-reduce(f32[]{:T(128)} %get-tuple-element.8), channel_id=1, replica_groups=mesh['gx'=16,'gy'=16] {'gx','gy'}, use_global_device_ids=true, to_apply=%region_10.11 | all-reduce | flops 1 | bytes 8 | tf_op jit(solution)/shard_map/psum | solution.py:141
  474.9 73.3 %psum.46 = f32[]{:T(128)} all-reduce(f32[]{:T(128)} %multiply_reduce_fusion), channel_id=1, replica_groups=mesh['gx'=16,'gy'=16] {'gx','gy'}, use_global_device_ids=true, to_apply=%region_12.13 | all-reduce | flops 1 | bytes 8 | tf_op jit(solution)/shard_map/psum | solution.py:63
  551.8 2.3 collective-permute-done.31
  556.0 1.8 collective-permute-start.33
  559.5 80.6 %psum.47 = f32[]{:T(128)} all-reduce(f32[]{:T(128)} %fusion.34), channel_id=1, replica_groups=mesh['gx'=16,'gy'=16] {'gx','gy'}, use_global_device_ids=true, to_apply=%region_14.15 | all-reduce | flops 1 | bytes 8 | tf_op jit(solution)/shard_map/psum | solution.py:141
  (127 shorter events, 32.8 us)
Async XLA Ops:
  1.6 6.6 %collective-permute-start = (bf16[4,2,16,2]{3,2,1,0:T(8,128)(2,1)S(1)}, bf16[4,2,16,2]{3,2,1,0:T(8,128)(2,1)S(1)}, u32[]{:S(2)}, u32[]{:S(2)}) collective-permute-start(bf16[4,2,16,2]{3,2,1,0:T(8,128)(2,1)S(1)} %get-tuple-element.34), channel_id=1, source_target_pairs={{0,16},{16,32},{32,48},{48,64},{64,80},{80,96},{96,112},{112,128},... | collective-permute-start | bytes 1544 | tf_op jit(solution)/shard_map/ppermute | solution.py:18
  4.2 4.0 collective-permute-start.1
  6.5 52.6 %collective-permute-start.12 = (f32[3,16,1]{2,1,0:T(8,128)S(1)}, f32[3,16,1]{2,1,0:T(8,128)S(1)}, u32[]{:S(2)}, u32[]{:S(2)}) collective-permute-start(f32[3,16,1]{2,1,0:T(8,128)S(1)} %get-tuple-element.42), channel_id=1, source_target_pairs={{0,16},{16,32},{32,48},{48,64},{64,80},{80,96},{96,112},{112,128},... | collective-permute-start | bytes 584 | tf_op jit(solution)/shard_map/ppermute | solution.py:18
  9.0 7.7 %collective-permute-start.2 = (bf16[4,2,2,132]{3,2,1,0:T(2,128)(2,1)S(1)}, bf16[4,2,2,132]{3,2,1,0:T(2,128)(2,1)S(1)}, u32[]{:S(2)}, u32[]{:S(2)}) collective-permute-start(bf16[4,2,2,132]{3,2,1,0:T(2,128)(2,1)S(1)} %get-tuple-element.28), channel_id=1, source_target_pairs={{0,1},{1,2},{2,3},{3,4},{4,5},{5,6},{6,7},{7,8},{8,9},{9,10},{10,1... | collective-permute-start | bytes 12680 | tf_op jit(solution)/shard_map/ppermute | solution.py:18
  10.8 6.0 collective-permute-start.3
  38.0 9.5 %collective-permute-start.4 = (bf16[8,128,16,2]{1,0,3,2:T(8,128)(2,1)S(1)}, bf16[8,128,16,2]{1,0,3,2:T(8,128)(2,1)S(1)}, u32[]{:S(2)}, u32[]{:S(2)}) collective-permute-start(bf16[8,128,16,2]{1,0,3,2:T(8,128)(2,1)S(1)} %get-tuple-element.26), channel_id=1, source_target_pairs={{0,16},{16,32},{32,48},{48,64},{64,80},{80,96},{96,112},{112,128},... | collective-permute-start | bytes 196616 | tf_op jit(solution)/shard_map/ppermute | solution.py:18
  39.0 8.5 %collective-permute-start.5 = (bf16[8,128,16,2]{1,0,3,2:T(8,128)(2,1)S(1)}, bf16[8,128,16,2]{1,0,3,2:T(8,128)(2,1)S(1)}, u32[]{:S(2)}, u32[]{:S(2)}) collective-permute-start(bf16[8,128,16,2]{1,0,3,2:T(8,128)(2,1)S(1)} %get-tuple-element.27), channel_id=1, source_target_pairs={{16,0},{32,16},{48,32},{64,48},{80,64},{96,80},{112,96},{128,112},... | collective-permute-start | bytes 196616 | tf_op jit(solution)/shard_map/ppermute | solution.py:21
  42.1 11.2 %collective-permute-start.18 = (f32[16,1]{1,0:T(8,128)S(1)}, f32[16,1]{1,0:T(8,128)S(1)}, u32[]{:S(2)}, u32[]{:S(2)}) collective-permute-start(f32[16,1]{1,0:T(8,128)S(1)} %get-tuple-element.52), channel_id=1, source_target_pairs={{0,16},{16,32},{32,48},{48,64},{64,80},{80,96},{96,112},{112,128},... | collective-permute-start | bytes 200 | tf_op jit(solution)/shard_map/ppermute | solution.py:18
  42.2 16.8 %collective-permute-start.19 = (f32[16,1]{1,0:T(8,128)S(1)}, f32[16,1]{1,0:T(8,128)S(1)}, u32[]{:S(2)}, u32[]{:S(2)}) collective-permute-start(f32[16,1]{1,0:T(8,128)S(1)} %get-tuple-element.53), channel_id=1, source_target_pairs={{16,0},{32,16},{48,32},{64,48},{80,64},{96,80},{112,96},{128,112},... | collective-permute-start | bytes 200 | tf_op jit(solution)/shard_map/ppermute | solution.py:21
  49.0 13.8 %collective-permute-start.6 = (bf16[8,128,2,132]{1,0,3,2:T(8,128)(2,1)S(1)}, bf16[8,128,2,132]{1,0,3,2:T(8,128)(2,1)S(1)}, u32[]{:S(2)}, u32[]{:S(2)}) collective-permute-start(bf16[8,128,2,132]{1,0,3,2:T(8,128)(2,1)S(1)} %get-tuple-element.20), channel_id=1, source_target_pairs={{0,1},{1,2},{2,3},{3,4},{4,5},{5,6},{6,7},{7,8},{8,9},{9,10},{10,1... | collective-permute-start | bytes 1622024 | tf_op jit(solution)/shard_map/ppermute | solution.py:18
  49.1 17.3 %collective-permute-start.7 = (bf16[8,128,2,132]{1,0,3,2:T(8,128)(2,1)S(1)}, bf16[8,128,2,132]{1,0,3,2:T(8,128)(2,1)S(1)}, u32[]{:S(2)}, u32[]{:S(2)}) collective-permute-start(bf16[8,128,2,132]{1,0,3,2:T(8,128)(2,1)S(1)} %get-tuple-element.21), channel_id=1, source_target_pairs={{1,0},{2,1},{3,2},{4,3},{5,4},{6,5},{7,6},{8,7},{9,8},{10,9},{11,1... | collective-permute-start | bytes 1622024 | tf_op jit(solution)/shard_map/ppermute | solution.py:21
  53.3 9.3 %collective-permute-start.13 = (f32[3,16,1]{2,1,0:T(8,128)S(1)}, f32[3,16,1]{2,1,0:T(8,128)S(1)}, u32[]{:S(2)}, u32[]{:S(2)}) collective-permute-start(f32[3,16,1]{2,1,0:T(8,128)S(1)} %get-tuple-element.43), channel_id=1, source_target_pairs={{16,0},{32,16},{48,32},{64,48},{80,64},{96,80},{112,96},{128,112},... | collective-permute-start | bytes 584 | tf_op jit(solution)/shard_map/ppermute | solution.py:21
  59.0 143.9 %collective-permute-start.20 = (f32[1,130]{1,0:T(1,128)S(1)}, f32[1,130]{1,0:T(1,128)S(1)}, u32[]{:S(2)}, u32[]{:S(2)}) collective-permute-start(f32[1,130]{1,0:T(1,128)S(1)} %get-tuple-element.44), channel_id=1, source_target_pairs={{0,1},{1,2},{2,3},{3,4},{4,5},{5,6},{6,7},{7,8},{8,9},{9,10},{10,1... | collective-permute-start | bytes 1568 | tf_op jit(solution)/shard_map/ppermute | solution.py:18
  59.0 143.8 %collective-permute-start.21 = (f32[1,130]{1,0:T(1,128)S(1)}, f32[1,130]{1,0:T(1,128)S(1)}, u32[]{:S(2)}, u32[]{:S(2)}) collective-permute-start(f32[1,130]{1,0:T(1,128)S(1)} %get-tuple-element.45), channel_id=1, source_target_pairs={{1,0},{2,1},{3,2},{4,3},{5,4},{6,5},{7,6},{8,7},{9,8},{10,9},{11,1... | collective-permute-start | bytes 1568 | tf_op jit(solution)/shard_map/ppermute | solution.py:21
  62.7 32.2 %collective-permute-start.14 = (f32[3,1,130]{2,1,0:T(1,128)S(1)}, f32[3,1,130]{2,1,0:T(1,128)S(1)}, u32[]{:S(2)}, u32[]{:S(2)}) collective-permute-start(f32[3,1,130]{2,1,0:T(1,128)S(1)} %get-tuple-element.30), channel_id=1, source_target_pairs={{0,1},{1,2},{2,3},{3,4},{4,5},{5,6},{6,7},{7,8},{8,9},{9,10},{10,1... | collective-permute-start | bytes 4688 | tf_op jit(solution)/shard_map/ppermute | solution.py:18
  62.8 35.3 %collective-permute-start.15 = (f32[3,1,130]{2,1,0:T(1,128)S(1)}, f32[3,1,130]{2,1,0:T(1,128)S(1)}, u32[]{:S(2)}, u32[]{:S(2)}) collective-permute-start(f32[3,1,130]{2,1,0:T(1,128)S(1)} %get-tuple-element.31), channel_id=1, source_target_pairs={{1,0},{2,1},{3,2},{4,3},{5,4},{6,5},{7,6},{8,7},{9,8},{10,9},{11,1... | collective-permute-start | bytes 4688 | tf_op jit(solution)/shard_map/ppermute | solution.py:21
  94.8 3.9 collective-permute-start.8
  94.9 4.1 collective-permute-start.9
  99.1 7.5 %collective-permute-start.10 = (bf16[8,64,1,130]{1,0,3,2:T(8,128)(2,1)S(1)}, bf16[8,64,1,130]{1,0,3,2:T(8,128)(2,1)S(1)}, u32[]{:S(2)}, u32[]{:S(2)}) collective-permute-start(bf16[8,64,1,130]{1,0,3,2:T(8,128)(2,1)S(1)} %get-tuple-element.22), channel_id=1, source_target_pairs={{0,1},{1,2},{2,3},{3,4},{4,5},{5,6},{6,7},{7,8},{8,9},{9,10},{10,1... | collective-permute-start | bytes 399368 | tf_op jit(solution)/shard_map/ppermute | solution.py:18
  99.1 7.5 %collective-permute-start.11 = (bf16[8,64,1,130]{1,0,3,2:T(8,128)(2,1)S(1)}, bf16[8,64,1,130]{1,0,3,2:T(8,128)(2,1)S(1)}, u32[]{:S(2)}, u32[]{:S(2)}) collective-permute-start(bf16[8,64,1,130]{1,0,3,2:T(8,128)(2,1)S(1)} %get-tuple-element.23), channel_id=1, source_target_pairs={{1,0},{2,1},{3,2},{4,3},{5,4},{6,5},{7,6},{8,7},{9,8},{10,9},{11,1... | collective-permute-start | bytes 399368 | tf_op jit(solution)/shard_map/ppermute | solution.py:21
  201.2 7.7 %collective-permute-start.16 = (f32[16,1]{1,0:T(8,128)S(1)}, f32[16,1]{1,0:T(8,128)S(1)}, u32[]{:S(2)}, u32[]{:S(2)}) collective-permute-start(f32[16,1]{1,0:T(8,128)S(1)} %slice.268), channel_id=1, source_target_pairs={{0,16},{16,32},{32,48},{48,64},{64,80},{80,96},{96,112},{112,128},... | collective-permute-start | bytes 200 | tf_op jit(solution)/shard_map/ppermute | solution.py:29
  201.6 7.3 %collective-permute-start.17 = (f32[1,128]{1,0:T(1,128)S(1)}, f32[1,128]{1,0:T(1,128)S(1)}, u32[]{:S(2)}, u32[]{:S(2)}) collective-permute-start(f32[1,128]{1,0:T(1,128)S(1)} %slice.272), channel_id=1, source_target_pairs={{0,1},{1,2},{2,3},{3,4},{4,5},{5,6},{6,7},{7,8},{8,9},{9,10},{10,1... | collective-permute-start | bytes 1544 | tf_op jit(solution)/shard_map/ppermute | solution.py:35
  209.1 6.7 %collective-permute-start.22 = (f32[16,1]{1,0:T(8,128)S(1)}, f32[16,1]{1,0:T(8,128)S(1)}, u32[]{:S(2)}, u32[]{:S(2)}) collective-permute-start(f32[16,1]{1,0:T(8,128)S(1)} %get-tuple-element.50), channel_id=1, source_target_pairs={{0,16},{16,32},{32,48},{48,64},{64,80},{80,96},{96,112},{112,128},... | collective-permute-start | bytes 200 | tf_op jit(solution)/shard_map/ppermute | solution.py:18
  209.1 6.9 %collective-permute-start.23 = (f32[16,1]{1,0:T(8,128)S(1)}, f32[16,1]{1,0:T(8,128)S(1)}, u32[]{:S(2)}, u32[]{:S(2)}) collective-permute-start(f32[16,1]{1,0:T(8,128)S(1)} %get-tuple-element.51), channel_id=1, source_target_pairs={{16,0},{32,16},{48,32},{64,48},{80,64},{96,80},{112,96},{128,112},... | collective-permute-start | bytes 200 | tf_op jit(solution)/shard_map/ppermute | solution.py:21
  216.1 5.1 collective-permute-start.24
  216.1 5.1 collective-permute-start.25
  383.9 3.1 collective-permute-start.27
  387.0 4.5 collective-permute-start.28
  388.8 2.8 collective-permute-start.29
  551.0 3.1 collective-permute-start.31
  554.2 4.5 collective-permute-start.32
  556.0 2.8 collective-permute-start.33
  (15 other events, 593.5 us)
where the time goes:
time: 647 us; the launch traced here: 642 us
  blocking collectives  392 us (61%)
  matrix products  124 us (19%)
  starting transfers between devices  66.4 us (10%)
  waiting for transfers between devices  21.4 us (3%)
  other arithmetic  15.9 us (2%)
  local copies, waits for them, and re-layouts  15 us (2%)
  between operations  7.81 us (1%)
    psum x3, blocking collectives, squares(): return lax.psum(jnp.sum(residual * residual), ('gx', 'gy'))  231 us
    psum x2, blocking collectives, body(): alpha = norm_now / lax.psum(jnp.sum(direction * image), ('gx', 'gy'))  161 us
    conv_general_dilated x3, matrix products, convolve(): lax.conv_general_dilated(field, kernel, (1, 1), 'VALID', dimension_number...  124 us
    ppermute x16, starting transfers between devices, with_halo(): lax.ppermute(lax.slice_in_dim(block, 0, width, axis=dim), axis, backward)  51.7 us
    ppermute x16, starting transfers between devices, with_halo(): lax.ppermute(lax.slice_in_dim(block, block.shape[dim] - width, None, axis...  13 us
  transfers between devices with their start and end apart: 34, of which 15 were waited for; matrix products, arithmetic and copies ran while one was open for 23% of the time, Pallas kernels for 0%

commit v1 on v0

v1 whole, which is shorter than its diff:
```python
import functools

import jax
import jax.numpy as jnp
from jax import lax
from jax.experimental import pallas as pl
from jax.experimental.pallas import tpu as pltpu
from jax.sharding import PartitionSpec as P

MESH = pl.DeviceIdType.MESH
F32 = jnp.float32
BF16 = jnp.bfloat16
KEEP_SCALE = 4.0 / 3.0

WAYS = ((1, 0), (-1, 0), (0, 1), (0, -1), (1, 1), (-1, 1), (1, -1), (-1, -1))

ROWS, COLS, LEVELS = 16, 128, 4
XO_V, XO_1, XO_2 = 42, 38, 34
M_V, M_1, M_2 = 16 * XO_V, 16 * XO_1, 16 * XO_2


def iota(shape, dim):
    return lax.broadcasted_iota(jnp.int32, shape, dim)


def dot_t(a, b):
    return lax.dot_general(a, b, (((1,), (1,)), ((), ())), preferred_element_type=F32)


def dot(a, b):
    return jnp.dot(a, b, preferred_element_type=F32)


def shift_lanes(x, by):
    return pltpu.roll(x, by % x.shape[1], 1)


def shift_rows(x, by):
    return pltpu.roll(x, by % x.shape[0], 0)


def kernel(
    nx,
    ny,
    vel,
    w1,
    b1,
    w2,
    b2,
    w3,
    b3,
    d1,
    d2,
    thick,
    eta,
    face,
    stor,
    ocean,
    f_out,
    e_out,
    v_rows,
    v_cols,
    v_corner,
    st_own,
    fx_own,
    rv_rows,
    rv_cols,
    rv_corner,
    rst_cols,
    rst_rows,
    rfx_cols,
    rfx_rows,
    red_a,
    red_b,
    got_a,
    got_b,
    vx,
    bmat,
    pick,
    umat,
    w1pad,
    w1all,
    w2all,
    w3f,
    h1,
    zacc,
    perm,
    v_send,
    v_recv,
    s_send,
    s_recv,
    x_send,
    x_recv,
    a_send,
    a_recv,
    b_send,
    b_recv,
):
    mx = lax.axis_index("gx")
    my = lax.axis_index("gy")

    def there(step_x, step_y):
        return (lax.rem(mx + step_x + nx, nx), lax.rem(my + step_y + ny, ny))

    barrier = pltpu.get_barrier_semaphore()
    peers = [there(k, 0) for k in range(1, nx)]
    peers += [there(0, k) for k in range(1, ny)]
    peers += [there(sx, sy) for sx, sy in WAYS[4:]]
    for peer in peers:
        pl.semaphore_signal(barrier, inc=1, device_id=peer, device_id_type=MESH)

    lane = iota((ROWS, COLS), 1)
    group = lane // 32
    low = lane % 32 < 16
    own = [[vel[l, c].astype(F32) for c in range(2)] for l in range(LEVELS)]
    for c in range(2):
        packed = None
        for l in range(LEVELS):
            first = own[l][c] if l == 0 else shift_lanes(own[l][c], 32 * l)
            last = own[l][c] if l == 3 else shift_lanes(own[l][c], 32 * (l + 1))
            both = jnp.where(low, first, last)
            packed = both if l == 0 else jnp.where(group == l, both, packed)
        v_cols[pl.ds(16 * c, 16), :] = packed.astype(BF16)
        if c == 0:
            packed_first = packed
    for side in range(2):
        cut = slice(8, 16) if side == 0 else slice(0, 8)
        rows = jnp.concatenate([own[l][c][cut] for l in range(LEVELS) for c in range(2)], axis=0)
        v_rows[side] = rows.astype(BF16)
        v_corner[side] = jnp.concatenate([packed_first[cut], packed[cut]], axis=0).astype(BF16)
    st_own[0] = eta[...]
    st_own[1] = face[0]
    st_own[2] = face[1]
    st_own[3] = stor[...]
    st_own[4] = ocean[...].astype(F32)

    pl.semaphore_wait(barrier, len(peers))

    copies_v, copies_s = [], []
    for d, (sx, sy) in enumerate(WAYS):
        side = 0 if sy == 1 else 1
        if sy == 0:
            src, dst = v_cols, rv_cols.at[d]
        elif sx == 0:
            src, dst = v_rows.at[side], rv_rows.at[d - 2]
        else:
            src, dst = v_corner.at[side], rv_corner.at[d - 4]
        copy = pltpu.make_async_remote_copy(
            src_ref=src,
            dst_ref=dst,
            send_sem=v_send.at[d],
            recv_sem=v_recv.at[d],
            device_id=there(sx, sy),
            device_id_type=MESH,
        )
        copy.start()
        copies_v.append(copy)
    for d, (sx, sy) in enumerate(WAYS):
        if sy == 0:
            src, dst = st_own, rst_cols.at[d]
        else:
            src = st_own.at[:, pl.ds(8 if sy == 1 else 0, 8), :]
            dst = rst_rows.at[d - 2]
        copy = pltpu.make_async_remote_copy(
            src_ref=src,
            dst_ref=dst,
            send_sem=s_send.at[d],
            recv_sem=s_recv.at[d],
            device_id=there(sx, sy),
            device_id_type=MESH,
        )
        copy.start()
        copies_s.append(copy)

    w1pad[...] = jnp.zeros_like(w1pad)
    for c in range(2):
        for dy in range(5):
            taps = w1[c, dy].astype(F32)
            for dx in range(5):
                w1pad[dx, c, pl.ds(10 + dy, 1), pl.ds(0, 128)] = taps[dx : dx + 1]
                w1pad[dx, c, pl.ds(11 + dy, 1), pl.ds(128, 128)] = taps[dx : dx + 1]
    for s in range(6):
        for dx in range(5):
            for c in range(2):
                block = w1pad[dx, c, pl.ds(10 - 2 * s, 16), :]
                w1all[s, pl.ds(32 * dx + 16 * c, 16), :] = block.astype(BF16)
        w1all[s, pl.ds(160, 96), :] = jnp.zeros((96, 256), BF16)

    kept = [d1[pl.ds(m, 1), :].astype(F32).astype(BF16) for m in range(2)]
    nothing = jnp.zeros((64, 128), BF16)
    for dx in range(5):
        for dy in range(-1, 6):
            for m in range(2):
                block = w2[dy, dx] * kept[m] if 0 <= dy < 5 else nothing
                for b in range(2):
                    if 0 <= dy + b < 6:
                        o, a = divmod(dy + b, 2)
                        w2all[pl.ds(128 * b + 64 * m, 64), pl.ds(((o * 5 + dx) * 2 + a) * 128, 128)] = block

    w3f[...] = jnp.zeros_like(w3f)
    for c in range(2):
        for ky in range(3):
            taps = w3[c, ky].astype(F32) * 0.5
            for dx in range(3):
                tap = taps[dx : dx + 1]
                both = jnp.concatenate([tap, tap], axis=1)
                for b in range(2):
                    w3f[pl.ds(8 * dx + 4 * c + b + 2 - ky, 1), pl.ds(128 * b, 128)] = both

    r = iota((M_V, 128), 0)
    lev = (r // 4) % 4
    x = 32 * (r % 4) + r // 16 - 5
    spot = jnp.where(x < 0, 512 + 32 * lev + 32 + x, jnp.where(x < 128, 128 * lev + x, 384 + 32 * lev + x))
    for k in range(5):
        pick[:, pl.ds(128 * k, 128)] = jnp.where(iota((M_V, 128), 1) + 128 * k == spot, 1.0, 0.0).astype(BF16)
    r = iota((512, 128), 0)
    spot = 128 * ((r // 4) % 4) + 32 * (r % 4) + r // 16
    for k in range(4):
        perm[:, pl.ds(128 * k, 128)] = jnp.where(iota((512, 128), 1) + 128 * k == spot, 1.0, 0.0).astype(BF16)

    has_south = jnp.where(my > 0, 1.0, 0.0)
    has_north = jnp.where(my < ny - 1, 1.0, 0.0)
    for copy in copies_v:
        copy.wait_recv()
    low8 = low[:8]
    south = rv_rows[0].astype(F32) * has_south
    north = rv_rows[1].astype(F32) * has_north
    from_w, from_e = rv_cols[0].astype(F32), rv_cols[1].astype(F32)
    from_sw, from_se = rv_corner[0].astype(F32), rv_corner[1].astype(F32)
    from_nw, from_ne = rv_corner[2].astype(F32), rv_corner[3].astype(F32)
    for c in range(2):
        for l in range(LEVELS):
            at = 8 * (2 * l + c)
            vx[l, c, pl.ds(0, 8), :] = south[at : at + 8]
            vx[l, c, pl.ds(8, 16), :] = own[l][c]
            vx[l, c, pl.ds(24, 8), :] = north[at : at + 8]
        cut = slice(8 * c, 8 * c + 8)
        vx[4, c, pl.ds(0, 8), :] = jnp.where(low8, from_se[cut], from_sw[cut]) * has_south
        cut16 = slice(16 * c, 16 * c + 16)
        vx[4, c, pl.ds(8, 16), :] = jnp.where(low, from_e[cut16], from_w[cut16])
        vx[4, c, pl.ds(24, 8), :] = jnp.where(low8, from_ne[cut], from_nw[cut]) * has_north
    for w in range(2):
        for k in range(5):
            for c in range(2):
                block = vx[k, c, pl.ds(3 + 10 * w, 16), :].astype(BF16)
                for rep in range(4):
                    bmat[pl.ds(128 * w + 32 * rep + 16 * c, 16), pl.ds(128 * k, 128)] = block
    umat[...] = dot_t(pick[...], bmat[...]).astype(BF16)

    bias1 = jnp.concatenate([b1[...].reshape(1, 128)] * 2, axis=1)
    upper = iota((1, 256), 1) // 128
    group1 = iota((M_1, 128), 1) // 32
    for w in range(2):
        lanes = pl.ds(128 * w, 128)
        near = umat[pl.ds(0, M_1), lanes]
        for g in range(1, 4):
            near = jnp.where(group1 == g, umat[pl.ds(16 * g, M_1), lanes], near)
        wide = jnp.concatenate([near, umat[pl.ds(64, M_1), lanes]], axis=1)

        def layer_one(j, carry, w=w, wide=wide):
            acc = dot(wide, w1all[j - 5 * w])
            row = my * ROWS + 2 * j - 3 + upper
            scale = jnp.where((row >= 0) & (row < ny * ROWS), KEEP_SCALE, 0.0)
            h1[j] = (jnp.maximum(acc + bias1, 0.0) * scale).astype(BF16)
            return carry

        lax.fori_loop(6 * w, 6 + 5 * w, layer_one, 0)

    bias2 = jnp.concatenate([b2[...].reshape(1, 64)] * 4, axis=1)
    keep2 = d2[...].astype(F32) * KEEP_SCALE
    keep2 = jnp.concatenate([keep2[0:1], keep2[1:2]] * 2, axis=1)
    zacc[...] = jnp.zeros_like(zacc)
    w3all = w3f[...].astype(BF16)

    def layer_two(n, carry):
        acc = None
        for o in range(3):
            for dx in range(5):
                left = h1[pl.ds(3 * n + o, 3), pl.ds(16 * dx, M_2), :].reshape(3 * M_2, 256)
                term = dot_t(left, w2all[:, pl.ds((o * 5 + dx) * 256, 256)])
                acc = term if acc is None else acc + term
        for q in range(3):
            i = 3 * n + q
            row = my * ROWS + 2 * i - 1 + upper
            scale = jnp.where((row >= 0) & (row < ny * ROWS), keep2, 0.0)
            hidden = (jnp.maximum(acc[M_2 * q : M_2 * (q + 1)] + bias2, 0.0) * scale).astype(BF16)
            z = dot_t(w3all, hidden)
            part = z[0:8, 0:512] + z[8:16, 16:528] + z[16:24, 32:544]
            for c in range(2):
                for t in range(4):
                    at = pl.ds(2 * i + t, 1)
                    zacc[c, at, :] = zacc[c, at, :] + part[4 * c + t : 4 * c + t + 1]
        return carry

    lax.fori_loop(0, 3, layer_two, 0)

    mixed = jnp.concatenate([zacc[0, pl.ds(2, 16), :], zacc[1, pl.ds(2, 16), :]], axis=0)
    high = mixed.astype(BF16)
    rest = (mixed - high.astype(F32)).astype(BF16)
    out = dot(jnp.concatenate([high, rest], axis=0), perm[...])
    out = out[0:32] + out[32:64]
    for c in range(2):
        total = None
        for l in range(LEVELS):
            forcing = out[16 * c : 16 * c + 16, 128 * l : 128 * l + 128] + b3[c]
            f_out[l, c] = forcing
            term = thick[l] * (vel[l, c].astype(F32) + forcing)
            total = term if total is None else total + term
        fx_own[c] = total

    copies_x = []
    for d, (sx, sy) in enumerate(WAYS):
        if sy == 0:
            src, dst = fx_own, rfx_cols.at[d]
        else:
            src = fx_own.at[:, pl.ds(8 if sy == 1 else 0, 8), :]
            dst = rfx_rows.at[d - 2]
        copy = pltpu.make_async_remote_copy(
            src_ref=src,
            dst_ref=dst,
            send_sem=x_send.at[d],
            recv_sem=x_recv.at[d],
            device_id=there(sx, sy),
            device_id_type=MESH,
        )
        copy.start()
        copies_x.append(copy)

    for copy in copies_s:
        copy.wait_recv()

    side = iota((ROWS, COLS), 1) < 64
    side8 = side[:8]

    def widened(own_ref, cols_ref, rows_ref, k):
        middle = jnp.concatenate([own_ref[k], jnp.where(side, cols_ref[1, k], cols_ref[0, k])], axis=1)
        below = jnp.concatenate([rows_ref[0, k], jnp.where(side8, rows_ref[3, k], rows_ref[2, k])], axis=1)
        above = jnp.concatenate([rows_ref[1, k], jnp.where(side8, rows_ref[5, k], rows_ref[4, k])], axis=1)
        return jnp.concatenate([below, middle, above], axis=0)

    eta_w, east_w, north_w, stor_w, sea = [widened(st_own, rst_cols, rst_rows, k) for k in range(5)]
    place = iota(sea.shape, 0) - 8 + my * ROWS
    sea = jnp.where((place >= 0) & (place < ny * ROWS), sea, 0.0)
    open_east = sea * shift_lanes(sea, -1)
    open_north = sea * shift_rows(sea, -1)
    coef_east = east_w * open_east
    coef_north = north_w * open_north
    coef_west = shift_lanes(coef_east, 1)
    coef_south = shift_rows(coef_north, 1)
    diagonal = stor_w + coef_east + coef_west + coef_north + coef_south

    def operate(field):
        return (
            diagonal * field
            - coef_east * shift_lanes(field, -1)
            - coef_west * shift_lanes(field, 1)
            - coef_north * shift_rows(field, -1)
            - coef_south * shift_rows(field, 1)
        )

    known = stor_w * eta_w - operate(eta_w)
    for copy in copies_x:
        copy.wait_recv()
    zonal, merid = [widened(fx_own, rfx_cols, rfx_rows, k) for k in range(2)]
    flux_east = zonal * open_east
    flux_north = merid * open_north
    diverge = flux_east - shift_lanes(flux_east, 1) + flux_north - shift_rows(flux_north, 1)
    k0 = known - diverge
    k1 = operate(k0)
    k2 = operate(k1)
    k3 = operate(k2)
    k0, k1, k2, k3 = [k[8:24, 0:128] for k in (k0, k1, k2, k3)]

    slot = iota((8, 128), 0)
    sums = jnp.zeros((8, 128), F32)
    for n, (a, b) in enumerate(((k0, k0), (k0, k1), (k1, k1), (k1, k2), (k2, k2), (k2, k3))):
        sums = jnp.where(slot == n, jnp.sum(a * b, axis=0, keepdims=True), sums)

    def exchange(values, mine, got, send, recv, count, target):
        mine[...] = values
        copies = []
        for k in range(1, count):
            copy = pltpu.make_async_remote_copy(
                src_ref=mine,
                dst_ref=got.at[k - 1],
                send_sem=send.at[k - 1],
                recv_sem=recv.at[k - 1],
                device_id=target(k),
                device_id_type=MESH,
            )
            copy.start()
            copies.append(copy)
        for copy in copies:
            copy.wait_recv()
        return values + jnp.sum(got[...], axis=0), copies

    sums, copies_a = exchange(sums, red_a, got_a, a_send, a_recv, nx, lambda k: there(k, 0))
    sums, copies_b = exchange(sums, red_b, got_b, b_send, b_recv, ny, lambda k: there(0, k))
    sums = jnp.sum(sums, axis=1, keepdims=True)
    m0, m1, m2, m3, m4, m5 = [jnp.broadcast_to(sums[n : n + 1], (1, 128)) for n in range(6)]

    def over(value, scale):
        fine = value > 1e-6 * scale
        return jnp.where(fine, 1.0 / jnp.where(fine, value, 1.0), 0.0)

    inv0 = over(m1, jnp.zeros_like(m1))
    l1 = m2 * inv0
    l2 = m3 * inv0
    p1 = m3 - l1 * m2
    inv1 = over(p1, m3)
    e21 = m4 - l2 * m2
    l21 = e21 * inv1
    p2 = m5 - l2 * m3 - l21 * e21
    inv2 = jnp.where(inv1 > 0.0, over(p2, m5), 0.0)
    z1 = m1 - l1 * m0
    z2 = m2 - l2 * m0 - l21 * z1
    c2 = z2 * inv2
    c1 = z1 * inv1 - l21 * c2
    c0 = m0 * inv0 - l1 * c1 - l2 * c2
    e_out[...] = eta[...] + c0 * k0 + c1 * k1 + c2 * k2

    for copy in copies_v + copies_s + copies_x + copies_a + copies_b:
        copy.wait_send()


def body(nx, ny, *args):
    vmem = pl.BlockSpec(memory_space=pltpu.VMEM)
    smem = pl.BlockSpec(memory_space=pltpu.SMEM)
    dma = pltpu.SemaphoreType.DMA
    V = pltpu.VMEM
    return pl.pallas_call(
        functools.partial(kernel, nx, ny),
        out_shape=(
            jax.ShapeDtypeStruct((LEVELS, 2, ROWS, COLS), F32),
            jax.ShapeDtypeStruct((ROWS, COLS), F32),
        ),
        in_specs=[vmem] * 6 + [smem] + [vmem] * 2 + [smem] + [vmem] * 4,
        out_specs=(vmem, vmem),
        scratch_shapes=[
            V((2, 64, 128), BF16),
            V((32, 128), BF16),
            V((2, 16, 128), BF16),
            V((5, ROWS, COLS), F32),
            V((2, ROWS, COLS), F32),
            V((2, 64, 128), BF16),
            V((2, 32, 128), BF16),
            V((4, 16, 128), BF16),
            V((2, 5, ROWS, COLS), F32),
            V((6, 5, 8, COLS), F32),
            V((2, 2, ROWS, COLS), F32),
            V((6, 2, 8, COLS), F32),
            V((8, 128), F32),
            V((8, 128), F32),
            V((nx - 1, 8, 128), F32),
            V((ny - 1, 8, 128), F32),
            V((5, 2, 32, 128), F32),
            V((256, 640), BF16),
            V((M_V, 640), BF16),
            V((M_V, 256), BF16),
            V((5, 2, 32, 256), F32),
            V((6, 256, 256), BF16),
            V((256, 3840), BF16),
            V((32, 256), F32),
            V((11, M_1, 256), BF16),
            V((2, 24, 512), F32),
            V((512, 512), BF16),
            dma((8,)),
            dma((8,)),
            dma((8,)),
            dma((8,)),
            dma((8,)),
            dma((8,)),
            dma((nx - 1,)),
            dma((nx - 1,)),
            dma((ny - 1,)),
            dma((ny - 1,)),
        ],
        compiler_params=pltpu.CompilerParams(
            collective_id=0, has_side_effects=True, vmem_limit_bytes=48 * 2**20
        ),
        name="ocean_step",
    )(*args)


def solution(mesh):
    nx, ny = mesh.shape["gx"], mesh.shape["gy"]
    tile = P("gy", "gx")
    stacked = P(None, "gy", "gx")
    levels = P(None, None, "gy", "gx")
    in_specs = (levels,) + (P(),) * 9 + (tile, stacked, tile, tile)
    return jax.shard_map(
        functools.partial(body, nx, ny),
        mesh=mesh,
        in_specs=in_specs,
        out_specs=(levels, tile),
        check_vma=False,
    )
```

time: 647 us -> 55.7 us (0.09)
  blocking collectives: 392 us -> 0 us
  matrix products: 124 us -> 0 us
  starting transfers between devices: 66.4 us -> 0 us
  Pallas kernels: 0 us -> 47.4 us
  waiting for transfers between devices: 21.4 us -> 0 us
  other arithmetic: 15.9 us -> 0 us
  local copies, waits for them, and re-layouts: 15 us -> 7.13 us
  between operations: 7.81 us -> 0.72 us
    psum x5 -> x0, blocking collectives: 392 us -> none  [the longest x3 231 us: squares(): return lax.psum(jnp.sum(residual * residual), ('gx', 'gy'))]
    conv_general_dilated x3 -> x0, matrix products: 124 us -> none  [convolve(): lax.conv_general_dilated(field, kernel, (1, 1), 'VALID', dimension_number...]
    ppermute x34 -> x0, starting transfers between devices: 66.4 us -> none  [the longest x16 51.7 us: with_halo(): lax.ppermute(lax.slice_in_dim(block, 0, width, axis=dim), axis, backward)]
    pallas_call x0 -> x1, Pallas kernels: none -> 47.4 us  [body(): pl.pallas_call(functools.partial(kernel, nx, ny), out_shape=(jax.ShapeDty...]
    ppermute x34 -> x0, waiting for transfers between devices: 21.4 us -> none  [the longest x16 10.3 us: with_halo(): lax.ppermute(lax.slice_in_dim(block, block.shape[dim] - width, None, axis...]
  transfers between devices with their start and end apart: 34 -> 0, of which waited for: 15 -> 0; matrix products, arithmetic and copies ran while one was open for 23% -> 0% of each run, Pallas kernels for 0% -> 0%
where the time goes in v1:
time: 55.7 us; the launch traced here: 55.3 us
  Pallas kernels  47.4 us (85%)
  local copies, waits for them, and re-layouts  7.13 us (13%)
  between operations  0.72 us (1%)
    pallas_call x1, Pallas kernels, body(): pl.pallas_call(functools.partial(kernel, nx, ny), out_shape=(jax.ShapeDty...  47.4 us
    unnamed x28, local copies, waits for them, and re-layouts  7.13 us

profile of v1, /device:TPU:1, one launch (start us, length us, event | category | flops | bytes accessed | tf_op | source)
XLA Modules:
  0.0 55.3 jit_solution(14168184973993398664)
XLA Ops:
  0.6 0.0 copy-start.1
  0.6 0.7 %copy.17.w3 = bf16[2,3,3,64]{3,2,1,0:T(4,128)(2,1)S(1)} copy(bf16[2,3,3,64]{3,0,2,1:T(2,128)(2,1)} %param.19) | data formatting | bytes 4608 | tf_op args[5]
  1.3 0.0 copy-start.3
  1.3 0.0 copy-start.6
  1.3 0.0 copy-start.7
  1.3 0.0 copy-start.8
  1.4 0.0 copy-start.9
  1.4 0.8 %copy.16.w1 = bf16[2,5,5,128]{3,2,1,0:T(8,128)(2,1)S(1)} copy(bf16[2,5,5,128]{3,0,2,1:T(2,128)(2,1)} %param.15) | data formatting | bytes 25600 | tf_op args[1]
  2.1 0.0 copy-done.1
  2.1 0.0 copy-done.3
  2.1 0.0 copy-done.6
  2.1 0.0 copy-done.7
  2.2 0.0 copy-done.8
  2.2 0.0 copy-done.9
  2.2 0.0 copy-start
  2.2 1.0 %copy-done = bf16[5,5,64,128]{3,2,1,0:T(8,128)(2,1)S(1)} copy-done((bf16[5,5,64,128]{3,2,1,0:T(8,128)(2,1)S(1)}, bf16[5,5,64,128]{3,2,1,0:T(8,128)(2,1)}, u32[]{:S(2)}) %copy-start) | copy-done | bytes 409624
  3.2 0.0 copy-start.2
  3.2 0.7 %copy-done.2 = f32[2,16,128]{2,1,0:T(8,128)S(1)} copy-done((f32[2,16,128]{2,1,0:T(8,128)S(1)}, f32[2,16,128]{2,1,0:T(8,128)}, u32[]{:S(2)}) %copy-start.2) | copy-done | bytes 16408
  3.9 0.0 copy-start.4
  3.9 0.7 %copy-done.4 = f32[16,128]{1,0:T(8,128)S(1)} copy-done((f32[16,128]{1,0:T(8,128)S(1)}, f32[16,128]{1,0:T(8,128)}, u32[]{:S(2)}) %copy-start.4) | copy-done | bytes 8216
  4.6 0.0 copy-start.5
  4.6 0.7 %copy-done.5 = s32[16,128]{1,0:T(8,128)S(1)} copy-done((s32[16,128]{1,0:T(8,128)S(1)}, s32[16,128]{1,0:T(8,128)}, u32[]{:S(2)}) %copy-start.5) | copy-done | bytes 8216
  5.3 0.0 copy-start.10
  5.3 0.7 %copy-done.10 = f32[2]{0:T(128)S(1)} copy-done((f32[2]{0:T(128)S(1)}, f32[2]{0:T(128)}, u32[]{:S(2)}) %copy-start.10) | copy-done | bytes 32
  6.0 0.0 copy-start.11
  6.0 0.7 %copy-done.11 = f32[4]{0:T(128)S(1)} copy-done((f32[4]{0:T(128)S(1)}, f32[4]{0:T(128)}, u32[]{:S(2)}) %copy-start.11) | copy-done | bytes 40
  6.6 47.4 %ocean_step.1 = (f32[4,2,16,128]{3,2,1,0:T(8,128)S(1)}, f32[16,128]{1,0:T(8,128)S(1)}) custom-call(bf16[4,2,16,128]{3,2,1,0:T(8,128)(2,1)S(1)} %copy-done.1, bf16[2,5,5,128]{3,2,1,0:T(8,128)(2,1)S(1)} %copy.16.w1, f32[128]{0:T(128)S(1)} %copy-done.8, bf16[5,5,64,128]{3,2,1,0:T(8,128)(2,1)S(1)} %copy-done, f32[64]{0:T(128)S(1)} %copy-done.9, ...), custom_call_target="tpu_custom_call" | custom-call | tf_op jit(solution)/shard_map/ocean_step/pallas_call | solution.py:431
  54.0 0.6 %copy.20 = f32[4,2,16,128]{3,2,1,0:T(8,128)} copy(f32[4,2,16,128]{3,2,1,0:T(8,128)S(1)} %get-tuple-element.4) | data formatting | bytes 131072
  54.7 0.6 %copy.21 = f32[16,128]{1,0:T(8,128)} copy(f32[16,128]{1,0:T(8,128)S(1)} %get-tuple-element.5) | data formatting | bytes 16384
Async XLA Ops:
  0.6 1.5 %copy-start.1 = (bf16[4,2,16,128]{3,2,1,0:T(8,128)(2,1)S(1)}, bf16[4,2,16,128]{3,2,1,0:T(8,128)(2,1)}, u32[]{:S(2)}) copy-start(bf16[4,2,16,128]{3,2,1,0:T(8,128)(2,1)} %vel.1) | copy-start | bytes 98308
  1.3 0.8 %copy-start.3 = (f32[16,128]{1,0:T(8,128)S(1)}, f32[16,128]{1,0:T(8,128)}, u32[]{:S(2)}) copy-start(f32[16,128]{1,0:T(8,128)} %eta.1) | copy-start | bytes 24580
  1.3 0.8 %copy-start.6 = (s32[2,128]{1,0:T(2,128)S(1)}, s32[2,128]{1,0:T(2,128)}, u32[]{:S(2)}) copy-start(s32[2,128]{1,0:T(2,128)} %d1.1) | copy-start | bytes 3076
  1.3 0.8 %copy-start.7 = (s32[2,64]{1,0:T(2,128)S(1)}, s32[2,64]{1,0:T(2,128)}, u32[]{:S(2)}) copy-start(s32[2,64]{1,0:T(2,128)} %d2.1) | copy-start | bytes 1540
  1.3 0.8 %copy-start.8 = (f32[128]{0:T(128)S(1)}, f32[128]{0:T(128)}, u32[]{:S(2)}) copy-start(f32[128]{0:T(128)} %b1.1) | copy-start | bytes 1540
  1.4 0.8 %copy-start.9 = (f32[64]{0:T(128)S(1)}, f32[64]{0:T(128)}, u32[]{:S(2)}) copy-start(f32[64]{0:T(128)} %b2.1) | copy-start | bytes 772
  2.2 1.0 %copy-start = (bf16[5,5,64,128]{3,2,1,0:T(8,128)(2,1)S(1)}, bf16[5,5,64,128]{3,2,1,0:T(8,128)(2,1)}, u32[]{:S(2)}) copy-start(bf16[5,5,64,128]{3,2,1,0:T(8,128)(2,1)} %w2.1) | copy-start | bytes 1228804
  3.2 0.7 %copy-start.2 = (f32[2,16,128]{2,1,0:T(8,128)S(1)}, f32[2,16,128]{2,1,0:T(8,128)}, u32[]{:S(2)}) copy-start(f32[2,16,128]{2,1,0:T(8,128)} %face.1) | copy-start | bytes 49156
  3.9 0.7 %copy-start.4 = (f32[16,128]{1,0:T(8,128)S(1)}, f32[16,128]{1,0:T(8,128)}, u32[]{:S(2)}) copy-start(f32[16,128]{1,0:T(8,128)} %stor.1) | copy-start | bytes 24580
  4.6 0.7 %copy-start.5 = (s32[16,128]{1,0:T(8,128)S(1)}, s32[16,128]{1,0:T(8,128)}, u32[]{:S(2)}) copy-start(s32[16,128]{1,0:T(8,128)} %ocean.1) | copy-start | bytes 24580
  5.3 0.7 %copy-start.10 = (f32[2]{0:T(128)S(1)}, f32[2]{0:T(128)}, u32[]{:S(2)}) copy-start(f32[2]{0:T(128)} %b3.1) | copy-start | bytes 28
  6.0 0.7 %copy-start.11 = (f32[4]{0:T(128)S(1)}, f32[4]{0:T(128)}, u32[]{:S(2)}) copy-start(f32[4]{0:T(128)} %thick.1) | copy-start | bytes 52

commit v2 on v1

--- a/solution.py
+++ b/solution.py
@@ -1,4 +1,5 @@
 import functools
+import itertools
 
 import jax
 import jax.numpy as jnp
@@ -15,7 +16,15 @@
 WAYS = ((1, 0), (-1, 0), (0, 1), (0, -1), (1, 1), (-1, 1), (1, -1), (-1, -1))
 
 ROWS, COLS, LEVELS = 16, 128, 4
+SEND_ORDER = (4, 5, 6, 7, 2, 3, 0, 1)
+
+SPLIT_X = ((2, 2), (4, 1), (2, 0))
+SPLIT_Y = ((2, 1), (8, 1))
+
+LOAD_ORDER = (0, 10, 11, 12, 13, 1, 7, 3, 5, 2, 4, 6, 8, 9)
+
 XO_V, XO_1, XO_2 = 42, 38, 34
+EDGE_W, EDGE_E = 5, 28
 M_V, M_1, M_2 = 16 * XO_V, 16 * XO_1, 16 * XO_2
 
 
@@ -29,6 +38,21 @@
 
 def dot(a, b):
     return jnp.dot(a, b, preferred_element_type=F32)
+
+
+def others(index, split):
+    sizes = [size for size, _ in split]
+    steps = list(itertools.product(*[range(size) for size in sizes]))[1:]
+    steps.sort(key=lambda step: -sum(hops * min(k, size - k) for k, (size, hops) in zip(step, split)))
+    found = []
+    for step in steps:
+        at, stride = 0, 1
+        for k, size in reversed(list(zip(step, sizes))):
+            digit = lax.rem(lax.div(index, jnp.int32(stride)), jnp.int32(size))
+            at = at + lax.rem(digit + k, jnp.int32(size)) * stride
+            stride *= size
+        found.append(at)
+    return found
 
 
 def shift_lanes(x, by):
@@ -42,60 +66,54 @@
 def kernel(
     nx,
     ny,
-    vel,
-    w1,
-    b1,
-    w2,
-    b2,
-    w3,
-    b3,
-    d1,
-    d2,
-    thick,
-    eta,
-    face,
-    stor,
-    ocean,
-    f_out,
-    e_out,
-    v_rows,
-    v_cols,
-    v_corner,
-    st_own,
-    fx_own,
-    rv_rows,
-    rv_cols,
-    rv_corner,
-    rst_cols,
-    rst_rows,
-    rfx_cols,
-    rfx_rows,
-    red_a,
-    red_b,
-    got_a,
-    got_b,
-    vx,
-    bmat,
-    pick,
-    umat,
-    w1pad,
-    w1all,
-    w2all,
-    w3f,
-    h1,
-    zacc,
-    perm,
-    v_send,
-    v_recv,
-    s_send,
-    s_recv,
-    x_send,
-    x_recv,
-    a_send,
-    a_recv,
-    b_send,
-    b_recv,
+    *refs,
 ):
+    given, refs = refs[:14], refs[14:]
+    (f_out, e_out), refs = refs[:2], refs[2:]
+    here, refs = refs[:14], refs[14:]
+    vel, w1, b1, w2, b2, w3, b3, d1, d2, thick, eta, face, stor, ocean = here
+    (
+        v_rows,
+        v_cols,
+        v_corner,
+        st_own,
+        fx_own,
+        fx_all,
+        rv_rows,
+        rv_cols,
+        rv_corner,
+        rst_cols,
+        rst_rows,
+        rfx_cols,
+        rfx_rows,
+        red_a,
+        red_b,
+        got_a,
+        got_b,
+        vx,
+        bmat,
+        pick,
+        umat,
+        w1pad,
+        w1all,
+        w2all,
+        w3f,
+        h1,
+        h2,
+        zacc,
+        perm,
+        v_send,
+        v_recv,
+        s_send,
+        s_recv,
+        x_send,
+        x_recv,
+        a_send,
+        a_recv,
+        b_send,
+        b_recv,
+        load_sem,
+    ) = refs
     mx = lax.axis_index("gx")
     my = lax.axis_index("gy")
 
@@ -103,11 +121,17 @@
         return (lax.rem(mx + step_x + nx, nx), lax.rem(my + step_y + ny, ny))
 
     barrier = pltpu.get_barrier_semaphore()
-    peers = [there(k, 0) for k in range(1, nx)]
-    peers += [there(0, k) for k in range(1, ny)]
-    peers += [there(sx, sy) for sx, sy in WAYS[4:]]
+    peers_x = [(at, my) for at in others(mx, SPLIT_X)]
+    peers_y = [(mx, at) for at in others(my, SPLIT_Y)]
+    peers = peers_x + peers_y + [there(sx, sy) for sx, sy in WAYS[4:]]
     for peer in peers:
         pl.semaphore_signal(barrier, inc=1, device_id=peer, device_id_type=MESH)
+
+    loads = [pltpu.make_async_copy(src, dst, load_sem.at[n]) for n, (src, dst) in enumerate(zip(given, here))]
+    for n in LOAD_ORDER:
+        loads[n].start()
+    for n in LOAD_ORDER[:5]:
+        loads[n].wait()
 
     lane = iota((ROWS, COLS), 1)
     group = lane // 32
@@ -137,7 +161,8 @@
     pl.semaphore_wait(barrier, len(peers))
 
     copies_v, copies_s = [], []
-    for d, (sx, sy) in enumerate(WAYS):
+    for d in SEND_ORDER:
+        sx, sy = WAYS[d]
         side = 0 if sy == 1 else 1
         if sy == 0:
             src, dst = v_cols, rv_cols.at[d]
@@ -155,7 +180,8 @@
         )
         copy.start()
         copies_v.append(copy)
-    for d, (sx, sy) in enumerate(WAYS):
+    for d in SEND_ORDER:
+        sx, sy = WAYS[d]
         if sy == 0:
             src, dst = st_own, rst_cols.at[d]
         else:
@@ -172,13 +198,15 @@
         copy.start()
         copies_s.append(copy)
 
+    for n in LOAD_ORDER[5:]:
+        loads[n].wait()
     w1pad[...] = jnp.zeros_like(w1pad)
-    for c in range(2):
-        for dy in range(5):
-            taps = w1[c, dy].astype(F32)
-            for dx in range(5):
-                w1pad[dx, c, pl.ds(10 + dy, 1), pl.ds(0, 128)] = taps[dx : dx + 1]
-                w1pad[dx, c, pl.ds(11 + dy, 1), pl.ds(128, 128)] = taps[dx : dx + 1]
+    for dy in range(5):
+        for dx in range(5):
+            taps = w1[dy, dx].astype(F32)
+            for c in range(2):
+                w1pad[dx, c, pl.ds(10 + dy, 1), pl.ds(0, 128)] = taps[c : c + 1]
+                w1pad[dx, c, pl.ds(11 + dy, 1), pl.ds(128, 128)] = taps[c : c + 1]
     for s in range(6):
         for dx in range(5):
             for c in range(2):
@@ -198,11 +226,11 @@
                         w2all[pl.ds(128 * b + 64 * m, 64), pl.ds(((o * 5 + dx) * 2 + a) * 128, 128)] = block
 
     w3f[...] = jnp.zeros_like(w3f)
-    for c in range(2):
-        for ky in range(3):
-            taps = w3[c, ky].astype(F32) * 0.5
-            for dx in range(3):
-                tap = taps[dx : dx + 1]
+    for ky in range(3):
+        for dx in range(3):
+            taps = w3[ky, dx].astype(F32) * 0.5
+            for c in range(2):
+                tap = taps[c : c + 1]
                 both = jnp.concatenate([tap, tap], axis=1)
                 for b in range(2):
                     w3f[pl.ds(8 * dx + 4 * c + b + 2 - ky, 1), pl.ds(128 * b, 128)] = both
@@ -272,44 +300,66 @@
     zacc[...] = jnp.zeros_like(zacc)
     w3all = w3f[...].astype(BF16)
 
-    def layer_two(n, carry):
+    def layer_two(first, spans):
         acc = None
         for o in range(3):
             for dx in range(5):
-                left = h1[pl.ds(3 * n + o, 3), pl.ds(16 * dx, M_2), :].reshape(3 * M_2, 256)
+                lefts = [
+                    h1[pl.ds(first + o, 3), pl.ds(16 * (dx + start), 16 * length), :].reshape(48 * length, 256)
+                    for start, length in spans
+                ]
+                left = lefts[0] if len(lefts) == 1 else jnp.concatenate(lefts, axis=0)
                 term = dot_t(left, w2all[:, pl.ds((o * 5 + dx) * 256, 256)])
                 acc = term if acc is None else acc + term
+        at = 0
+        for start, length in spans:
+            for q in range(3):
+                row = my * ROWS + 2 * (first + q) - 1 + upper
+                scale = jnp.where((row >= 0) & (row < ny * ROWS), keep2, 0.0)
+                hidden = jnp.maximum(acc[at : at + 16 * length] + bias2, 0.0) * scale
+                h2[first + q, pl.ds(16 * start, 16 * length), :] = hidden.astype(BF16)
+                at += 16 * length
+
+    def layer_three(target, first):
         for q in range(3):
-            i = 3 * n + q
-            row = my * ROWS + 2 * i - 1 + upper
-            scale = jnp.where((row >= 0) & (row < ny * ROWS), keep2, 0.0)
-            hidden = (jnp.maximum(acc[M_2 * q : M_2 * (q + 1)] + bias2, 0.0) * scale).astype(BF16)
-            z = dot_t(w3all, hidden)
+            z = dot_t(w3all, h2[first + q])
             part = z[0:8, 0:512] + z[8:16, 16:528] + z[16:24, 32:544]
             for c in range(2):
                 for t in range(4):
-                    at = pl.ds(2 * i + t, 1)
-                    zacc[c, at, :] = zacc[c, at, :] + part[4 * c + t : 4 * c + t + 1]
+                    at = pl.ds(2 * (first + q) + t, 1)
+                    zacc[target, c, at, :] = zacc[target, c, at, :] + part[4 * c + t : 4 * c + t + 1]
+
+    def finish(mixed, fx, f):
+        high = mixed.astype(BF16)
+        rest = (mixed - high.astype(F32)).astype(BF16)
+        out = dot(jnp.concatenate([high, rest], axis=0), perm[...])
+        out = out[0:32] + out[32:64]
+        for c in range(2):
+            total = None
+            for l in range(LEVELS):
+                forcing = out[16 * c : 16 * c + 16, 128 * l : 128 * l + 128] + b3[c]
+                if f is not None:
+                    f[l, c] = forcing
+                term = thick[l] * (vel[l, c].astype(F32) + forcing)
+                total = term if total is None else total + term
+            fx[c] = total
+
+    def outer_rows(n, carry):
+        layer_two(6 * n, [(0, XO_2)])
         return carry
 
-    lax.fori_loop(0, 3, layer_two, 0)
-
-    mixed = jnp.concatenate([zacc[0, pl.ds(2, 16), :], zacc[1, pl.ds(2, 16), :]], axis=0)
-    high = mixed.astype(BF16)
-    rest = (mixed - high.astype(F32)).astype(BF16)
-    out = dot(jnp.concatenate([high, rest], axis=0), perm[...])
-    out = out[0:32] + out[32:64]
-    for c in range(2):
-        total = None
-        for l in range(LEVELS):
-            forcing = out[16 * c : 16 * c + 16, 128 * l : 128 * l + 128] + b3[c]
-            f_out[l, c] = forcing
-            term = thick[l] * (vel[l, c].astype(F32) + forcing)
-            total = term if total is None else total + term
-        fx_own[c] = total
+    lax.fori_loop(0, 2, outer_rows, 0)
+    h2[pl.ds(3, 3), pl.ds(16 * EDGE_W, 16 * (EDGE_E - EDGE_W)), :] = jnp.zeros((3, 16 * (EDGE_E - EDGE_W), 256), BF16)
+    layer_two(3, [(0, EDGE_W), (EDGE_E, XO_2 - EDGE_E)])
+    layer_three(0, 0)
+    layer_three(0, 6)
+    layer_three(1, 3)
+    sums01 = [zacc[0, c, pl.ds(2, 16), :] + zacc[1, c, pl.ds(2, 16), :] for c in range(2)]
+    finish(jnp.concatenate(sums01, axis=0), fx_own, None)
 
     copies_x = []
-    for d, (sx, sy) in enumerate(WAYS):
+    for d in SEND_ORDER:
+        sx, sy = WAYS[d]
         if sy == 0:
             src, dst = fx_own, rfx_cols.at[d]
         else:
@@ -326,6 +376,11 @@
         copy.start()
         copies_x.append(copy)
 
+    layer_two(3, [(EDGE_W, EDGE_E - EDGE_W)])
+    layer_three(2, 3)
+    sums02 = [zacc[0, c, pl.ds(2, 16), :] + zacc[2, c, pl.ds(2, 16), :] for c in range(2)]
+    finish(jnp.concatenate(sums02, axis=0), fx_all, f_out)
+
     for copy in copies_s:
         copy.wait_recv()
 
@@ -361,7 +416,7 @@
     known = stor_w * eta_w - operate(eta_w)
     for copy in copies_x:
         copy.wait_recv()
-    zonal, merid = [widened(fx_own, rfx_cols, rfx_rows, k) for k in range(2)]
+    zonal, merid = [widened(fx_all, rfx_cols, rfx_rows, k) for k in range(2)]
     flux_east = zonal * open_east
     flux_north = merid * open_north
     diverge = flux_east - shift_lanes(flux_east, 1) + flux_north - shift_rows(flux_north, 1)
@@ -371,21 +426,22 @@
     k3 = operate(k2)
     k0, k1, k2, k3 = [k[8:24, 0:128] for k in (k0, k1, k2, k3)]
 
-    slot = iota((8, 128), 0)
-    sums = jnp.zeros((8, 128), F32)
+    lane1 = iota((1, 128), 1)
+    sums = jnp.zeros((1, 128), F32)
     for n, (a, b) in enumerate(((k0, k0), (k0, k1), (k1, k1), (k1, k2), (k2, k2), (k2, k3))):
-        sums = jnp.where(slot == n, jnp.sum(a * b, axis=0, keepdims=True), sums)
-
-    def exchange(values, mine, got, send, recv, count, target):
+        total = jnp.sum(jnp.sum(a * b, axis=0, keepdims=True), axis=1, keepdims=True)
+        sums = jnp.where(lane1 == n, total, sums)
+
+    def exchange(values, mine, got, send, recv, targets):
         mine[...] = values
         copies = []
-        for k in range(1, count):
+        for k, target in enumerate(targets):
             copy = pltpu.make_async_remote_copy(
                 src_ref=mine,
-                dst_ref=got.at[k - 1],
-                send_sem=send.at[k - 1],
-                recv_sem=recv.at[k - 1],
-                device_id=target(k),
+                dst_ref=got.at[k],
+                send_sem=send.at[k],
+                recv_sem=recv.at[k],
+                device_id=target,
                 device_id_type=MESH,
             )
             copy.start()
@@ -394,10 +450,11 @@
             copy.wait_recv()
         return values + jnp.sum(got[...], axis=0), copies
 
-    sums, copies_a = exchange(sums, red_a, got_a, a_send, a_recv, nx, lambda k: there(k, 0))
-    sums, copies_b = exchange(sums, red_b, got_b, b_send, b_recv, ny, lambda k: there(0, k))
-    sums = jnp.sum(sums, axis=1, keepdims=True)
-    m0, m1, m2, m3, m4, m5 = [jnp.broadcast_to(sums[n : n + 1], (1, 128)) for n in range(6)]
+    sums, copies_a = exchange(sums, red_a, got_a, a_send, a_recv, peers_x)
+    sums, copies_b = exchange(sums, red_b, got_b, b_send, b_recv, peers_y)
+    m0, m1, m2, m3, m4, m5 = [
+        jnp.sum(jnp.where(lane1 == n, sums, 0.0), axis=1, keepdims=True) for n in range(6)
+    ]
 
     def over(value, scale):
         fine = value > 1e-6 * scale
@@ -425,7 +482,10 @@
 
 def body(nx, ny, *args):
     vmem = pl.BlockSpec(memory_space=pltpu.VMEM)
-    smem = pl.BlockSpec(memory_space=pltpu.SMEM)
+    args = list(args)
+    args[1] = jnp.transpose(args[1], (1, 2, 0, 3))
+    args[5] = jnp.transpose(args[5], (1, 2, 0, 3))
+    here = [(pltpu.SMEM if n in (6, 9) else pltpu.VMEM)(a.shape, a.dtype) for n, a in enumerate(args)]
     dma = pltpu.SemaphoreType.DMA
     V = pltpu.VMEM
     return pl.pallas_call(
@@ -434,13 +494,14 @@
             jax.ShapeDtypeStruct((LEVELS, 2, ROWS, COLS), F32),
             jax.ShapeDtypeStruct((ROWS, COLS), F32),
         ),
-        in_specs=[vmem] * 6 + [smem] + [vmem] * 2 + [smem] + [vmem] * 4,
+        in_specs=[pl.BlockSpec(memory_space=pltpu.HBM)] * 14,
         out_specs=(vmem, vmem),
-        scratch_shapes=[
+        scratch_shapes=here + [
             V((2, 64, 128), BF16),
             V((32, 128), BF16),
             V((2, 16, 128), BF16),
             V((5, ROWS, COLS), F32),
+            V((2, ROWS, COLS), F32),
             V((2, ROWS, COLS), F32),
             V((2, 64, 128), BF16),
             V((2, 32, 128), BF16),
@@ -449,10 +510,10 @@
             V((6, 5, 8, COLS), F32),
             V((2, 2, ROWS, COLS), F32),
             V((6, 2, 8, COLS), F32),
-            V((8, 128), F32),
-            V((8, 128), F32),
-            V((nx - 1, 8, 128), F32),
-            V((ny - 1, 8, 128), F32),
+            V((1, 128), F32),
+            V((1, 128), F32),
+            V((nx - 1, 1, 128), F32),
+            V((ny - 1, 1, 128), F32),
             V((5, 2, 32, 128), F32),
             V((256, 640), BF16),
             V((M_V, 640), BF16),
@@ -462,7 +523,8 @@
             V((256, 3840), BF16),
             V((32, 256), F32),
             V((11, M_1, 256), BF16),
-            V((2, 24, 512), F32),
+            V((9, M_2, 256), BF16),
+            V((3, 2, 24, 512), F32),
             V((512, 512), BF16),
             dma((8,)),
             dma((8,)),
@@ -474,9 +536,10 @@
             dma((nx - 1,)),
             dma((ny - 1,)),
             dma((ny - 1,)),
+            dma((14,)),
         ],
         compiler_params=pltpu.CompilerParams(
-            collective_id=0, has_side_effects=True, vmem_limit_bytes=48 * 2**20
+            collective_id=0, has_side_effects=True, vmem_limit_bytes=60 * 2**20
         ),
         name="ocean_step",
     )(*args)

time: 55.7 us -> 47 us (0.84)
  local copies, waits for them, and re-layouts: 7.13 us -> 2.08 us
  Pallas kernels: 47.4 us -> 44.2 us
    unnamed x28 -> x4, local copies, waits for them, and re-layouts: 7.13 us -> 2.08 us
    pallas_call x1, Pallas kernels: 47.4 us -> 44.2 us  [body(): pl.pallas_call(functools.partial(kernel, nx, ny), out_shape=(jax.ShapeDty...]
where the time goes in v2:
time: 47 us; the launch traced here: 46.9 us
  Pallas kernels  44.2 us (94%)
  local copies, waits for them, and re-layouts  2.08 us (4%)
  between operations  0.65 us (1%)
    pallas_call x1, Pallas kernels, body(): pl.pallas_call(functools.partial(kernel, nx, ny), out_shape=(jax.ShapeDty...  44.2 us
    unnamed x4, local copies, waits for them, and re-layouts  2.08 us

profile of v2, /device:TPU:1, one launch (start us, length us, event | category | flops | bytes accessed | tf_op | source)
XLA Modules:
  0.0 46.9 jit_solution(14042121867122395874)
XLA Ops:
  0.6 44.2 %ocean_step.1 = (f32[4,2,16,128]{3,2,1,0:T(8,128)}, f32[16,128]{1,0:T(8,128)}) custom-call(bf16[4,2,16,128]{3,2,1,0:T(8,128)(2,1)} %refs_0_.1, bf16[5,5,2,128]{3,2,1,0:T(2,128)(2,1)} %bitcast.2, f32[128]{0:T(128)} %refs_2_.1, bf16[5,5,64,128]{3,2,1,0:T(8,128)(2,1)} %refs_3_.1, f32[64]{0:T(128)} %refs_4_.1, bf16[3,3,2,64]{3,2,1,0:T(2,128)(2,1)} %bitcast.3, ...), custom_call_target="tpu_custom_call" | custom-call | tf_op jit(solution)/shard_map/ocean_step/pallas_call | solution.py:491
  44.8 0.0 copy-start
  44.8 1.5 %copy.18 = f32[4,2,16,128]{3,2,1,0:T(8,128)} copy(f32[4,2,16,128]{3,2,1,0:T(8,128)} %get-tuple-element.4) | data formatting | bytes 131072
  46.3 0.0 copy-done
  46.3 0.6 %copy.19 = f32[16,128]{1,0:T(8,128)} copy(f32[16,128]{1,0:T(8,128)S(1)} %copy-done) | data formatting | bytes 16384
Async XLA Ops:
  44.8 1.5 %copy-start = (f32[16,128]{1,0:T(8,128)S(1)}, f32[16,128]{1,0:T(8,128)}, u32[]{:S(2)}) copy-start(f32[16,128]{1,0:T(8,128)} %get-tuple-element.5) | copy-start | bytes 24580

commit v3 on v2

--- a/solution.py
+++ b/solution.py
@@ -101,6 +101,7 @@
         h1,
         h2,
         zacc,
+        mixed_out,
         perm,
         v_send,
         v_recv,
@@ -123,15 +124,14 @@
     barrier = pltpu.get_barrier_semaphore()
     peers_x = [(at, my) for at in others(mx, SPLIT_X)]
     peers_y = [(mx, at) for at in others(my, SPLIT_Y)]
-    peers = peers_x + peers_y + [there(sx, sy) for sx, sy in WAYS[4:]]
+    peers = [there(sx, sy) for sx, sy in WAYS[4:]] + peers_x[::-1] + peers_y[::-1]
+    loads = [pltpu.make_async_copy(src, dst, load_sem.at[n]) for n, (src, dst) in enumerate(zip(given, here))]
+    loads[0].start()
     for peer in peers:
         pl.semaphore_signal(barrier, inc=1, device_id=peer, device_id_type=MESH)
-
-    loads = [pltpu.make_async_copy(src, dst, load_sem.at[n]) for n, (src, dst) in enumerate(zip(given, here))]
-    for n in LOAD_ORDER:
+    for n in LOAD_ORDER[1:]:
         loads[n].start()
-    for n in LOAD_ORDER[:5]:
-        loads[n].wait()
+    loads[0].wait()
 
     lane = iota((ROWS, COLS), 1)
     group = lane // 32
@@ -152,11 +152,6 @@
         rows = jnp.concatenate([own[l][c][cut] for l in range(LEVELS) for c in range(2)], axis=0)
         v_rows[side] = rows.astype(BF16)
         v_corner[side] = jnp.concatenate([packed_first[cut], packed[cut]], axis=0).astype(BF16)
-    st_own[0] = eta[...]
-    st_own[1] = face[0]
-    st_own[2] = face[1]
-    st_own[3] = stor[...]
-    st_own[4] = ocean[...].astype(F32)
 
     pl.semaphore_wait(barrier, len(peers))
 
@@ -180,6 +175,13 @@
         )
         copy.start()
         copies_v.append(copy)
+    for n in LOAD_ORDER[1:5]:
+        loads[n].wait()
+    st_own[0] = eta[...]
+    st_own[1] = face[0]
+    st_own[2] = face[1]
+    st_own[3] = stor[...]
+    st_own[4] = ocean[...].astype(F32)
     for d in SEND_ORDER:
         sx, sy = WAYS[d]
         if sy == 0:
@@ -233,7 +235,7 @@
                 tap = taps[c : c + 1]
                 both = jnp.concatenate([tap, tap], axis=1)
                 for b in range(2):
-                    w3f[pl.ds(8 * dx + 4 * c + b + 2 - ky, 1), pl.ds(128 * b, 128)] = both
+                    w3f[pl.ds(8 * dx + 2 * (b + 2 - ky) + c, 1), pl.ds(128 * b, 128)] = both
 
     r = iota((M_V, 128), 0)
     lev = (r // 4) % 4
@@ -285,19 +287,15 @@
             near = jnp.where(group1 == g, umat[pl.ds(16 * g, M_1), lanes], near)
         wide = jnp.concatenate([near, umat[pl.ds(64, M_1), lanes]], axis=1)
 
-        def layer_one(j, carry, w=w, wide=wide):
+        for j in range(6 * w, 6 + 5 * w):
             acc = dot(wide, w1all[j - 5 * w])
             row = my * ROWS + 2 * j - 3 + upper
             scale = jnp.where((row >= 0) & (row < ny * ROWS), KEEP_SCALE, 0.0)
             h1[j] = (jnp.maximum(acc + bias1, 0.0) * scale).astype(BF16)
-            return carry
-
-        lax.fori_loop(6 * w, 6 + 5 * w, layer_one, 0)
 
     bias2 = jnp.concatenate([b2[...].reshape(1, 64)] * 4, axis=1)
     keep2 = d2[...].astype(F32) * KEEP_SCALE
     keep2 = jnp.concatenate([keep2[0:1], keep2[1:2]] * 2, axis=1)
-    zacc[...] = jnp.zeros_like(zacc)
     w3all = w3f[...].astype(BF16)
 
     def layer_two(first, spans):
@@ -320,24 +318,23 @@
                 h2[first + q, pl.ds(16 * start, 16 * length), :] = hidden.astype(BF16)
                 at += 16 * length
 
-    def layer_three(target, first):
-        for q in range(3):
-            z = dot_t(w3all, h2[first + q])
-            part = z[0:8, 0:512] + z[8:16, 16:528] + z[16:24, 32:544]
-            for c in range(2):
-                for t in range(4):
-                    at = pl.ds(2 * (first + q) + t, 1)
-                    zacc[target, c, at, :] = zacc[target, c, at, :] + part[4 * c + t : 4 * c + t + 1]
-
-    def finish(mixed, fx, f):
+    def layer_three(first):
+        for i in range(first, first + 3):
+            z = dot_t(w3all, h2[i])
+            zacc[i] = z[0:8, 0:512] + z[8:16, 16:528] + z[16:24, 32:544]
+
+    def finish(fx, f):
+        mixed = jnp.concatenate([zacc[p, pl.ds(4, 4), :] + zacc[p + 1, pl.ds(0, 4), :] for p in range(8)], axis=0)
         high = mixed.astype(BF16)
         rest = (mixed - high.astype(F32)).astype(BF16)
         out = dot(jnp.concatenate([high, rest], axis=0), perm[...])
-        out = out[0:32] + out[32:64]
+        for l in range(LEVELS):
+            lanes = slice(128 * l, 128 * l + 128)
+            mixed_out[l] = out[0:32, lanes] + out[32:64, lanes]
         for c in range(2):
             total = None
             for l in range(LEVELS):
-                forcing = out[16 * c : 16 * c + 16, 128 * l : 128 * l + 128] + b3[c]
+                forcing = mixed_out[l, pl.ds(c, 16, stride=2), :] + b3[c]
                 if f is not None:
                     f[l, c] = forcing
                 term = thick[l] * (vel[l, c].astype(F32) + forcing)
@@ -351,11 +348,10 @@
     lax.fori_loop(0, 2, outer_rows, 0)
     h2[pl.ds(3, 3), pl.ds(16 * EDGE_W, 16 * (EDGE_E - EDGE_W)), :] = jnp.zeros((3, 16 * (EDGE_E - EDGE_W), 256), BF16)
     layer_two(3, [(0, EDGE_W), (EDGE_E, XO_2 - EDGE_E)])
-    layer_three(0, 0)
-    layer_three(0, 6)
-    layer_three(1, 3)
-    sums01 = [zacc[0, c, pl.ds(2, 16), :] + zacc[1, c, pl.ds(2, 16), :] for c in range(2)]
-    finish(jnp.concatenate(sums01, axis=0), fx_own, None)
+    layer_three(0)
+    layer_three(6)
+    layer_three(3)
+    finish(fx_own, None)
 
     copies_x = []
     for d in SEND_ORDER:
@@ -377,9 +373,8 @@
         copies_x.append(copy)
 
     layer_two(3, [(EDGE_W, EDGE_E - EDGE_W)])
-    layer_three(2, 3)
-    sums02 = [zacc[0, c, pl.ds(2, 16), :] + zacc[2, c, pl.ds(2, 16), :] for c in range(2)]
-    finish(jnp.concatenate(sums02, axis=0), fx_all, f_out)
+    layer_three(3)
+    finish(fx_all, f_out)
 
     for copy in copies_s:
         copy.wait_recv()
@@ -491,8 +486,8 @@
     return pl.pallas_call(
         functools.partial(kernel, nx, ny),
         out_shape=(
-            jax.ShapeDtypeStruct((LEVELS, 2, ROWS, COLS), F32),
-            jax.ShapeDtypeStruct((ROWS, COLS), F32),
+            pltpu.VMEM((LEVELS, 2, ROWS, COLS), F32),
+            pltpu.VMEM((ROWS, COLS), F32),
         ),
         in_specs=[pl.BlockSpec(memory_space=pltpu.HBM)] * 14,
         out_specs=(vmem, vmem),
@@ -524,7 +519,8 @@
             V((32, 256), F32),
             V((11, M_1, 256), BF16),
             V((9, M_2, 256), BF16),
-            V((3, 2, 24, 512), F32),
+            V((9, 8, 512), F32),
+            V((LEVELS, 32, 128), F32),
             V((512, 512), BF16),
             dma((8,)),
             dma((8,)),

time: 47 us -> 44.2 us (0.940)
  Pallas kernels: 44.2 us -> 42.2 us
  local copies, waits for them, and re-layouts: 2.08 us -> 1.23 us
    pallas_call x1, Pallas kernels: 44.2 us -> 42.2 us  [body(): pl.pallas_call(functools.partial(kernel, nx, ny), out_shape=(pltpu.VMEM((...]
    unnamed x4 -> x2, local copies, waits for them, and re-layouts: 2.08 us -> 1.23 us
where the time goes in v3:
time: 44.2 us; the launch traced here: 44 us
  Pallas kernels  42.2 us (95%)
  local copies, waits for them, and re-layouts  1.23 us (3%)
  between operations  0.64 us (1%)
    pallas_call x1, Pallas kernels, body(): pl.pallas_call(functools.partial(kernel, nx, ny), out_shape=(pltpu.VMEM((...  42.2 us
    unnamed x2, local copies, waits for them, and re-layouts  1.23 us

profile of v3, /device:TPU:1, one launch (start us, length us, event | category | flops | bytes accessed | tf_op | source)
XLA Modules:
  0.0 44.0 jit_solution(10024428759934018357)
XLA Ops:
  0.6 42.2 %ocean_step.1 = (f32[4,2,16,128]{3,2,1,0:T(8,128)S(1)}, f32[16,128]{1,0:T(8,128)S(1)}) custom-call(bf16[4,2,16,128]{3,2,1,0:T(8,128)(2,1)} %refs_0_.1, bf16[5,5,2,128]{3,2,1,0:T(2,128)(2,1)} %bitcast.2, f32[128]{0:T(128)} %refs_2_.1, bf16[5,5,64,128]{3,2,1,0:T(8,128)(2,1)} %refs_3_.1, f32[64]{0:T(128)} %refs_4_.1, bf16[3,3,2,64]{3,2,1,0:T(2,128)(2,1)} %bitcast.3, ...), custom_call_target="tpu_custom_call" | custom-call | tf_op jit(solution)/shard_map/ocean_step/pallas_call | solution.py:486
  42.8 0.6 %copy.18 = f32[4,2,16,128]{3,2,1,0:T(8,128)} copy(f32[4,2,16,128]{3,2,1,0:T(8,128)S(1)} %get-tuple-element.2) | data formatting | bytes 131072
  43.4 0.6 %copy.19 = f32[16,128]{1,0:T(8,128)} copy(f32[16,128]{1,0:T(8,128)S(1)} %get-tuple-element.3) | data formatting | bytes 16384

commit v4 on v3

--- a/solution.py
+++ b/solution.py
@@ -24,7 +24,8 @@
 LOAD_ORDER = (0, 10, 11, 12, 13, 1, 7, 3, 5, 2, 4, 6, 8, 9)
 
 XO_V, XO_1, XO_2 = 42, 38, 34
-EDGE_W, EDGE_E = 5, 28
+U_2 = XO_2 // 2
+EDGE_W, EDGE_E = 3, 14
 M_V, M_1, M_2 = 16 * XO_V, 16 * XO_1, 16 * XO_2
 
 
@@ -99,6 +100,7 @@
         w2all,
         w3f,
         h1,
+        mixed1,
         h2,
         zacc,
         mixed_out,
@@ -175,6 +177,58 @@
         )
         copy.start()
         copies_v.append(copy)
+    for n in LOAD_ORDER[5:]:
+        loads[n].wait()
+    w1pad[...] = jnp.zeros_like(w1pad)
+    for dy in range(5):
+        for dx in range(5):
+            taps = w1[dy, dx].astype(F32)
+            for c in range(2):
+                w1pad[dx, c, pl.ds(10 + dy, 1), pl.ds(0, 128)] = taps[c : c + 1]
+                w1pad[dx, c, pl.ds(11 + dy, 1), pl.ds(128, 128)] = taps[c : c + 1]
+    for s in range(6):
+        for dx in range(5):
+            for c in range(2):
+                block = w1pad[dx, c, pl.ds(10 - 2 * s, 16), :]
+                w1all[s, pl.ds(32 * dx + 16 * c, 16), :] = block.astype(BF16)
+        w1all[s, pl.ds(160, 96), :] = jnp.zeros((96, 256), BF16)
+
+    kept = [d1[pl.ds(m, 1), :].astype(F32).astype(BF16) for m in range(2)]
+    nothing = jnp.zeros((64, 128), BF16)
+    for dy in range(-1, 6):
+        if 0 <= dy < 5:
+            g = [w2[dy, dx].astype(F32) for dx in range(5)]
+            mixes = [g[0], g[3], g[2], g[4], (g[0] + g[1] + g[2]) * 0.5, g[3] + g[4], (g[0] - g[1] + g[2]) * 0.5]
+            mixes = [mix.astype(BF16) for mix in mixes]
+        for n in range(7):
+            for m in range(2):
+                block = mixes[n] * kept[m] if 0 <= dy < 5 else nothing
+                for b in range(2):
+                    if 0 <= dy + b < 6:
+                        o, a = divmod(dy + b, 2)
+                        w2all[pl.ds(128 * b + 64 * m, 64), pl.ds(((n * 3 + o) * 2 + a) * 128, 128)] = block
+
+    w3f[...] = jnp.zeros_like(w3f)
+    for ky in range(3):
+        for dx in range(3):
+            taps = w3[ky, dx].astype(F32) * 0.5
+            for c in range(2):
+                tap = taps[c : c + 1]
+                both = jnp.concatenate([tap, tap], axis=1)
+                for b in range(2):
+                    w3f[pl.ds(8 * dx + 2 * (b + 2 - ky) + c, 1), pl.ds(128 * b, 128)] = both
+
+    r = iota((M_V, 128), 0)
+    lev = (r // 4) % 4
+    x = 32 * (r % 4) + r // 16 - 5
+    spot = jnp.where(x < 0, 512 + 32 * lev + 32 + x, jnp.where(x < 128, 128 * lev + x, 384 + 32 * lev + x))
+    for k in range(5):
+        pick[:, pl.ds(128 * k, 128)] = jnp.where(iota((M_V, 128), 1) + 128 * k == spot, 1.0, 0.0).astype(BF16)
+    r = iota((512, 128), 0)
+    spot = 128 * ((r // 4) % 4) + 32 * (r % 4) + r // 16
+    for k in range(4):
+        perm[:, pl.ds(128 * k, 128)] = jnp.where(iota((512, 128), 1) + 128 * k == spot, 1.0, 0.0).astype(BF16)
+
     for n in LOAD_ORDER[1:5]:
         loads[n].wait()
     st_own[0] = eta[...]
@@ -199,54 +253,6 @@
         )
         copy.start()
         copies_s.append(copy)
-
-    for n in LOAD_ORDER[5:]:
-        loads[n].wait()
-    w1pad[...] = jnp.zeros_like(w1pad)
-    for dy in range(5):
-        for dx in range(5):
-            taps = w1[dy, dx].astype(F32)
-            for c in range(2):
-                w1pad[dx, c, pl.ds(10 + dy, 1), pl.ds(0, 128)] = taps[c : c + 1]
-                w1pad[dx, c, pl.ds(11 + dy, 1), pl.ds(128, 128)] = taps[c : c + 1]
-    for s in range(6):
-        for dx in range(5):
-            for c in range(2):
-                block = w1pad[dx, c, pl.ds(10 - 2 * s, 16), :]
-                w1all[s, pl.ds(32 * dx + 16 * c, 16), :] = block.astype(BF16)
-        w1all[s, pl.ds(160, 96), :] = jnp.zeros((96, 256), BF16)
-
-    kept = [d1[pl.ds(m, 1), :].astype(F32).astype(BF16) for m in range(2)]
-    nothing = jnp.zeros((64, 128), BF16)
-    for dx in range(5):
-        for dy in range(-1, 6):
-            for m in range(2):
-                block = w2[dy, dx] * kept[m] if 0 <= dy < 5 else nothing
-                for b in range(2):
-                    if 0 <= dy + b < 6:
-                        o, a = divmod(dy + b, 2)
-                        w2all[pl.ds(128 * b + 64 * m, 64), pl.ds(((o * 5 + dx) * 2 + a) * 128, 128)] = block
-
-    w3f[...] = jnp.zeros_like(w3f)
-    for ky in range(3):
-        for dx in range(3):
-            taps = w3[ky, dx].astype(F32) * 0.5
-            for c in range(2):
-                tap = taps[c : c + 1]
-                both = jnp.concatenate([tap, tap], axis=1)
-                for b in range(2):
-                    w3f[pl.ds(8 * dx + 2 * (b + 2 - ky) + c, 1), pl.ds(128 * b, 128)] = both
-
-    r = iota((M_V, 128), 0)
-    lev = (r // 4) % 4
-    x = 32 * (r % 4) + r // 16 - 5
-    spot = jnp.where(x < 0, 512 + 32 * lev + 32 + x, jnp.where(x < 128, 128 * lev + x, 384 + 32 * lev + x))
-    for k in range(5):
-        pick[:, pl.ds(128 * k, 128)] = jnp.where(iota((M_V, 128), 1) + 128 * k == spot, 1.0, 0.0).astype(BF16)
-    r = iota((512, 128), 0)
-    spot = 128 * ((r // 4) % 4) + 32 * (r % 4) + r // 16
-    for k in range(4):
-        perm[:, pl.ds(128 * k, 128)] = jnp.where(iota((512, 128), 1) + 128 * k == spot, 1.0, 0.0).astype(BF16)
 
     has_south = jnp.where(my > 0, 1.0, 0.0)
     has_north = jnp.where(my < ny - 1, 1.0, 0.0)
@@ -291,7 +297,12 @@
             acc = dot(wide, w1all[j - 5 * w])
             row = my * ROWS + 2 * j - 3 + upper
             scale = jnp.where((row >= 0) & (row < ny * ROWS), KEEP_SCALE, 0.0)
-            h1[j] = (jnp.maximum(acc + bias1, 0.0) * scale).astype(BF16)
+            hidden = (jnp.maximum(acc + bias1, 0.0) * scale).astype(BF16)
+            h1[j] = hidden.reshape(XO_1 // 2, 32, 256)
+            d = [h1[j, pl.ds(k // 2, U_2), pl.ds(16 * (k % 2), 16), :] for k in range(6)]
+            mixes = (d[0] - d[2], d[3] - d[4], d[3] - d[1], d[5] - d[4], d[1] + d[2], d[2] - d[1])
+            for n, mix in enumerate(mixes):
+                mixed1[n, j] = mix
 
     bias2 = jnp.concatenate([b2[...].reshape(1, 64)] * 4, axis=1)
     keep2 = d2[...].astype(F32) * KEEP_SCALE
@@ -299,28 +310,38 @@
     w3all = w3f[...].astype(BF16)
 
     def layer_two(first, spans):
-        acc = None
-        for o in range(3):
-            for dx in range(5):
-                lefts = [
-                    h1[pl.ds(first + o, 3), pl.ds(16 * (dx + start), 16 * length), :].reshape(48 * length, 256)
-                    for start, length in spans
-                ]
+        def product(n):
+            total = None
+            for o in range(3):
+                lefts = []
+                for start, length in spans:
+                    if n == 5:
+                        left = h1[pl.ds(first + o, 3), pl.ds(start + 2, length), pl.ds(0, 16), :]
+                    else:
+                        left = mixed1[min(n, 5), pl.ds(first + o, 3), pl.ds(start, length), :, :]
+                    lefts.append(left.reshape(48 * length, 256))
                 left = lefts[0] if len(lefts) == 1 else jnp.concatenate(lefts, axis=0)
-                term = dot_t(left, w2all[:, pl.ds((o * 5 + dx) * 256, 256)])
-                acc = term if acc is None else acc + term
+                term = dot_t(left, w2all[:, pl.ds((n * 3 + o) * 256, 256)])
+                total = term if total is None else total + term
+            return total
+
+        both = product(4) + product(5)
+        half = product(6)
+        even = product(0) + product(1) + (both + half)
+        odd = product(2) + product(3) + (both - half)
         at = 0
         for start, length in spans:
             for q in range(3):
                 row = my * ROWS + 2 * (first + q) - 1 + upper
                 scale = jnp.where((row >= 0) & (row < ny * ROWS), keep2, 0.0)
-                hidden = jnp.maximum(acc[at : at + 16 * length] + bias2, 0.0) * scale
-                h2[first + q, pl.ds(16 * start, 16 * length), :] = hidden.astype(BF16)
+                for e, acc in enumerate((even, odd)):
+                    hidden = jnp.maximum(acc[at : at + 16 * length] + bias2, 0.0) * scale
+                    h2[first + q, pl.ds(start, length), pl.ds(16 * e, 16), :] = hidden.astype(BF16).reshape(length, 16, 256)
                 at += 16 * length
 
     def layer_three(first):
         for i in range(first, first + 3):
-            z = dot_t(w3all, h2[i])
+            z = dot_t(w3all, h2[i].reshape(M_2, 256))
             zacc[i] = z[0:8, 0:512] + z[8:16, 16:528] + z[16:24, 32:544]
 
     def finish(fx, f):
@@ -342,12 +363,12 @@
             fx[c] = total
 
     def outer_rows(n, carry):
-        layer_two(6 * n, [(0, XO_2)])
+        layer_two(6 * n, [(0, U_2)])
         return carry
 
     lax.fori_loop(0, 2, outer_rows, 0)
-    h2[pl.ds(3, 3), pl.ds(16 * EDGE_W, 16 * (EDGE_E - EDGE_W)), :] = jnp.zeros((3, 16 * (EDGE_E - EDGE_W), 256), BF16)
-    layer_two(3, [(0, EDGE_W), (EDGE_E, XO_2 - EDGE_E)])
+    h2[pl.ds(3, 3), pl.ds(EDGE_W, EDGE_E - EDGE_W), :, :] = jnp.zeros((3, EDGE_E - EDGE_W, 32, 256), BF16)
+    layer_two(3, [(0, EDGE_W), (EDGE_E, U_2 - EDGE_E)])
     layer_three(0)
     layer_three(6)
     layer_three(3)
@@ -515,10 +536,11 @@
             V((M_V, 256), BF16),
             V((5, 2, 32, 256), F32),
             V((6, 256, 256), BF16),
-            V((256, 3840), BF16),
+            V((256, 7 * 768), BF16),
             V((32, 256), F32),
-            V((11, M_1, 256), BF16),
-            V((9, M_2, 256), BF16),
+            V((11, XO_1 // 2, 32, 256), BF16),
+            V((6, 11, U_2, 16, 256), BF16),
+            V((9, U_2, 32, 256), BF16),
             V((9, 8, 512), F32),
             V((LEVELS, 32, 128), F32),
             V((512, 512), BF16),

time: 44.2 us -> 41.1 us (0.930)
  Pallas kernels: 42.2 us -> 39.1 us
    pallas_call x1, Pallas kernels: 42.2 us -> 39.1 us  [body(): pl.pallas_call(functools.partial(kernel, nx, ny), out_shape=(pltpu.VMEM((...]
where the time goes in v4:
time: 41.1 us; the launch traced here: 41 us
  Pallas kernels  39.1 us (95%)
  local copies, waits for them, and re-layouts  1.23 us (3%)
  between operations  0.64 us (2%)
    pallas_call x1, Pallas kernels, body(): pl.pallas_call(functools.partial(kernel, nx, ny), out_shape=(pltpu.VMEM((...  39.1 us
    unnamed x2, local copies, waits for them, and re-layouts  1.23 us

profile of v4, /device:TPU:1, one launch (start us, length us, event | category | flops | bytes accessed | tf_op | source)
XLA Modules:
  0.0 41.0 jit_solution(6150181035258372595)
XLA Ops:
  0.6 39.1 %ocean_step.1 = (f32[4,2,16,128]{3,2,1,0:T(8,128)S(1)}, f32[16,128]{1,0:T(8,128)S(1)}) custom-call(bf16[4,2,16,128]{3,2,1,0:T(8,128)(2,1)} %refs_0_.1, bf16[5,5,2,128]{3,2,1,0:T(2,128)(2,1)} %bitcast.2, f32[128]{0:T(128)} %refs_2_.1, bf16[5,5,64,128]{3,2,1,0:T(8,128)(2,1)} %refs_3_.1, f32[64]{0:T(128)} %refs_4_.1, bf16[3,3,2,64]{3,2,1,0:T(2,128)(2,1)} %bitcast.3, ...), custom_call_target="tpu_custom_call" | custom-call | tf_op jit(solution)/shard_map/ocean_step/pallas_call | solution.py:507
  39.8 0.6 %copy.18 = f32[4,2,16,128]{3,2,1,0:T(8,128)} copy(f32[4,2,16,128]{3,2,1,0:T(8,128)S(1)} %get-tuple-element.2) | data formatting | bytes 131072
  40.4 0.6 %copy.19 = f32[16,128]{1,0:T(8,128)} copy(f32[16,128]{1,0:T(8,128)S(1)} %get-tuple-element.3) | data formatting | bytes 16384

commit v5 on v4

--- a/solution.py
+++ b/solution.py
@@ -195,11 +195,16 @@
 
     kept = [d1[pl.ds(m, 1), :].astype(F32).astype(BF16) for m in range(2)]
     nothing = jnp.zeros((64, 128), BF16)
+    left4 = left5 = jnp.zeros((64, 128), F32)
     for dy in range(-1, 6):
         if 0 <= dy < 5:
             g = [w2[dy, dx].astype(F32) for dx in range(5)]
-            mixes = [g[0], g[3], g[2], g[4], (g[0] + g[1] + g[2]) * 0.5, g[3] + g[4], (g[0] - g[1] + g[2]) * 0.5]
+            sum4 = (g[0] + g[1] + g[2]) * 0.5 + left4
+            sum5 = g[3] + g[4] + left5
+            mixes = [g[0], g[3], g[2], g[4], sum4, sum5, (g[0] - g[1] + g[2]) * 0.5]
             mixes = [mix.astype(BF16) for mix in mixes]
+            left4 = sum4 - mixes[4].astype(F32)
+            left5 = sum5 - mixes[5].astype(F32)
         for n in range(7):
             for m in range(2):
                 block = mixes[n] * kept[m] if 0 <= dy < 5 else nothing
@@ -310,9 +315,9 @@
     w3all = w3f[...].astype(BF16)
 
     def layer_two(first, spans):
-        def product(n):
+        def product(*which):
             total = None
-            for o in range(3):
+            for n, o in itertools.product(which, range(3)):
                 lefts = []
                 for start, length in spans:
                     if n == 5:
@@ -325,10 +330,9 @@
                 total = term if total is None else total + term
             return total
 
-        both = product(4) + product(5)
-        half = product(6)
-        even = product(0) + product(1) + (both + half)
-        odd = product(2) + product(3) + (both - half)
+        both, half = product(4, 5), product(6)
+        even = product(0, 1) + (both + half)
+        odd = product(2, 3) + (both - half)
         at = 0
         for start, length in spans:
             for q in range(3):
@@ -362,11 +366,8 @@
                 total = term if total is None else total + term
             fx[c] = total
 
-    def outer_rows(n, carry):
-        layer_two(6 * n, [(0, U_2)])
-        return carry
-
-    lax.fori_loop(0, 2, outer_rows, 0)
+    layer_two(0, [(0, U_2)])
+    layer_two(6, [(0, U_2)])
     h2[pl.ds(3, 3), pl.ds(EDGE_W, EDGE_E - EDGE_W), :, :] = jnp.zeros((3, EDGE_E - EDGE_W, 32, 256), BF16)
     layer_two(3, [(0, EDGE_W), (EDGE_E, U_2 - EDGE_E)])
     layer_three(0)

time: 41.1 us -> 40.2 us (0.978)
  Pallas kernels: 39.1 us -> 38.2 us
    pallas_call x1, Pallas kernels: 39.1 us -> 38.2 us  [body(): pl.pallas_call(functools.partial(kernel, nx, ny), out_shape=(pltpu.VMEM((...]
where the time goes in v5:
time: 40.2 us; the launch traced here: 40.1 us
  Pallas kernels  38.2 us (95%)
  local copies, waits for them, and re-layouts  1.23 us (3%)
  between operations  0.64 us (2%)
    pallas_call x1, Pallas kernels, body(): pl.pallas_call(functools.partial(kernel, nx, ny), out_shape=(pltpu.VMEM((...  38.2 us
    unnamed x2, local copies, waits for them, and re-layouts  1.23 us

profile of v5, /device:TPU:1, one launch (start us, length us, event | category | flops | bytes accessed | tf_op | source)
XLA Modules:
  0.0 40.1 jit_solution(9073330258637311574)
XLA Ops:
  0.6 38.2 %ocean_step.1 = (f32[4,2,16,128]{3,2,1,0:T(8,128)S(1)}, f32[16,128]{1,0:T(8,128)S(1)}) custom-call(bf16[4,2,16,128]{3,2,1,0:T(8,128)(2,1)} %refs_0_.1, bf16[5,5,2,128]{3,2,1,0:T(2,128)(2,1)} %bitcast.2, f32[128]{0:T(128)} %refs_2_.1, bf16[5,5,64,128]{3,2,1,0:T(8,128)(2,1)} %refs_3_.1, f32[64]{0:T(128)} %refs_4_.1, bf16[3,3,2,64]{3,2,1,0:T(2,128)(2,1)} %bitcast.3, ...), custom_call_target="tpu_custom_call" | custom-call | tf_op jit(solution)/shard_map/ocean_step/pallas_call | solution.py:508
  38.8 0.6 %copy.18 = f32[4,2,16,128]{3,2,1,0:T(8,128)} copy(f32[4,2,16,128]{3,2,1,0:T(8,128)S(1)} %get-tuple-element.2) | data formatting | bytes 131072
  39.5 0.6 %copy.19 = f32[16,128]{1,0:T(8,128)} copy(f32[16,128]{1,0:T(8,128)S(1)} %get-tuple-element.3) | data formatting | bytes 16384

commit v6 on v5

--- a/solution.py
+++ b/solution.py
@@ -199,12 +199,12 @@
     for dy in range(-1, 6):
         if 0 <= dy < 5:
             g = [w2[dy, dx].astype(F32) for dx in range(5)]
-            sum4 = (g[0] + g[1] + g[2]) * 0.5 + left4
-            sum5 = g[3] + g[4] + left5
-            mixes = [g[0], g[3], g[2], g[4], sum4, sum5, (g[0] - g[1] + g[2]) * 0.5]
+            sum4 = g[0] + g[1] + left4
+            sum5 = g[2] + g[3] + left5
+            mixes = [g[0], g[2], g[1], g[3], g[4], sum4, sum5]
             mixes = [mix.astype(BF16) for mix in mixes]
-            left4 = sum4 - mixes[4].astype(F32)
-            left5 = sum5 - mixes[5].astype(F32)
+            left4 = sum4 - mixes[5].astype(F32)
+            left5 = sum5 - mixes[6].astype(F32)
         for n in range(7):
             for m in range(2):
                 block = mixes[n] * kept[m] if 0 <= dy < 5 else nothing
@@ -304,8 +304,8 @@
             scale = jnp.where((row >= 0) & (row < ny * ROWS), KEEP_SCALE, 0.0)
             hidden = (jnp.maximum(acc + bias1, 0.0) * scale).astype(BF16)
             h1[j] = hidden.reshape(XO_1 // 2, 32, 256)
-            d = [h1[j, pl.ds(k // 2, U_2), pl.ds(16 * (k % 2), 16), :] for k in range(6)]
-            mixes = (d[0] - d[2], d[3] - d[4], d[3] - d[1], d[5] - d[4], d[1] + d[2], d[2] - d[1])
+            d = [h1[j, pl.ds(k // 2, U_2), pl.ds(16 * (k % 2), 16), :] for k in range(5)]
+            mixes = (d[0] - d[1], d[2] - d[3], d[2] - d[1], d[4] - d[3])
             for n, mix in enumerate(mixes):
                 mixed1[n, j] = mix
 
@@ -317,22 +317,22 @@
     def layer_two(first, spans):
         def product(*which):
             total = None
-            for n, o in itertools.product(which, range(3)):
+            for (n, k), o in itertools.product(which, range(3)):
                 lefts = []
                 for start, length in spans:
-                    if n == 5:
-                        left = h1[pl.ds(first + o, 3), pl.ds(start + 2, length), pl.ds(0, 16), :]
+                    if k is None:
+                        left = mixed1[n, pl.ds(first + o, 3), pl.ds(start, length), :, :]
                     else:
-                        left = mixed1[min(n, 5), pl.ds(first + o, 3), pl.ds(start, length), :, :]
+                        left = h1[pl.ds(first + o, 3), pl.ds(start + k // 2, length), pl.ds(16 * (k % 2), 16), :]
                     lefts.append(left.reshape(48 * length, 256))
                 left = lefts[0] if len(lefts) == 1 else jnp.concatenate(lefts, axis=0)
                 term = dot_t(left, w2all[:, pl.ds((n * 3 + o) * 256, 256)])
                 total = term if total is None else total + term
             return total
 
-        both, half = product(4, 5), product(6)
-        even = product(0, 1) + (both + half)
-        odd = product(2, 3) + (both - half)
+        both = product((5, 1), (6, 3))
+        even = product((0, None), (1, None), (4, 4)) + both
+        odd = product((2, None), (3, None), (4, 5)) + both
         at = 0
         for start, length in spans:
             for q in range(3):
@@ -540,7 +540,7 @@
             V((256, 7 * 768), BF16),
             V((32, 256), F32),
             V((11, XO_1 // 2, 32, 256), BF16),
-            V((6, 11, U_2, 16, 256), BF16),
+            V((4, 11, U_2, 16, 256), BF16),
             V((9, U_2, 32, 256), BF16),
             V((9, 8, 512), F32),
             V((LEVELS, 32, 128), F32),

time: 40.2 us -> 40.9 us (1.017)
  Pallas kernels: 38.2 us -> 38.9 us
    pallas_call x1, Pallas kernels: 38.2 us -> 38.9 us  [body(): pl.pallas_call(functools.partial(kernel, nx, ny), out_shape=(pltpu.VMEM((...]
where the time goes in v6:
time: 40.9 us; the launch traced here: 40.8 us
  Pallas kernels  38.9 us (95%)
  local copies, waits for them, and re-layouts  1.23 us (3%)
  between operations  0.64 us (2%)
    pallas_call x1, Pallas kernels, body(): pl.pallas_call(functools.partial(kernel, nx, ny), out_shape=(pltpu.VMEM((...  38.9 us
    unnamed x2, local copies, waits for them, and re-layouts  1.23 us

profile of v6, /device:TPU:1, one launch (start us, length us, event | category | flops | bytes accessed | tf_op | source)
XLA Modules:
  0.0 40.8 jit_solution(8911813540516648415)
XLA Ops:
  0.6 38.9 %ocean_step.1 = (f32[4,2,16,128]{3,2,1,0:T(8,128)S(1)}, f32[16,128]{1,0:T(8,128)S(1)}) custom-call(bf16[4,2,16,128]{3,2,1,0:T(8,128)(2,1)} %refs_0_.1, bf16[5,5,2,128]{3,2,1,0:T(2,128)(2,1)} %bitcast.2, f32[128]{0:T(128)} %refs_2_.1, bf16[5,5,64,128]{3,2,1,0:T(8,128)(2,1)} %refs_3_.1, f32[64]{0:T(128)} %refs_4_.1, bf16[3,3,2,64]{3,2,1,0:T(2,128)(2,1)} %bitcast.3, ...), custom_call_target="tpu_custom_call" | custom-call | tf_op jit(solution)/shard_map/ocean_step/pallas_call | solution.py:508
  39.6 0.6 %copy.18 = f32[4,2,16,128]{3,2,1,0:T(8,128)} copy(f32[4,2,16,128]{3,2,1,0:T(8,128)S(1)} %get-tuple-element.2) | data formatting | bytes 131072
  40.2 0.6 %copy.19 = f32[16,128]{1,0:T(8,128)} copy(f32[16,128]{1,0:T(8,128)S(1)} %get-tuple-element.3) | data formatting | bytes 16384
